TPU v7x, 512 devices: a whole 4x8x8 slice. The times are simulated.
512 devices in a mesh: gx: 16 (over z, x_hi), gy: 16 (over y, core), band: 2 (over x_lo).
Axes of the slice: x: 4 (x_hi: 2, x_lo: 2; x = x_hi * 2 + x_lo), y: 8, z: 8, core: 2. Of those that a mesh axis runs over, the one named last changes fastest.
Arguments:
- orbitals: float32 [2, 4, 256, 256, 128], P(None, 'band', 'gx', 'gy'), may hold values from -6 to 6
- potential: float32 [256, 256, 128], P('gx', 'gy'), may hold values from -2 to 2
- corners: int32 [1024, 3], P(('gx', 'gy')), may hold values from 0 to 255, as said below
- counts: int32 [1024], P(('gx', 'gy')), may hold values from 1 to 4, as said below
- coupling: float32 [1024, 4, 4], P(('gx', 'gy')), may hold values from -7.5 to 7.5
- projectors: float32 [4, 4096], replicated
- occupations: float32 [4], P('band'), may hold values from 0.05 to 0.4
Outputs:
- propagated: float32 [2, 4, 256, 256, 128], P(None, 'band', 'gx', 'gy')
- density: float32 [256, 256, 128], P('gx', 'gy')
Inputs may be any that keep to these rules, and one draw needn't show every extreme that they name: An atom held by the pencil at index i of gx and j of gy has corners[a,0] in [i * 16, (i + 1) * 16) and corners[a,1] in [j * 16, (j + 1) * 16); every pencil holds an atom with x offset 16 - 1 in its pencil and one with y offset 16 - 1. `counts`: every pencil's atoms take each count from 1 to 4.
All inputs are finite; a program needn't handle non-finite values.
Results may differ from a plain program's by a relative error of at most 0.0001.
Values sent between devices are 32-bit elements; how exact they have to be, the bound alone decides.
A program may use at most 128 MiB of HBM per device.

v0:
```python
import jax
import jax.numpy as jnp
from jax import lax
from jax.sharding import PartitionSpec as P

BOX = 16
NPROJ = 4


time_step = 0.12
center_weight = -2.5
near_weight = 4.0 / 3.0
far_weight = -1.0 / 12.0
highest = lax.Precision.HIGHEST


def passed_along(block, axis, distance):
    devices = range(lax.axis_size(axis))
    route = [((i - distance) % len(devices), i) for i in devices]
    return lax.ppermute(block, axis, route)


def padded_2(block, sides, width):
    for axis, dim in sides:
        count = lax.axis_size(axis)
        forward = [(i, i + 1) for i in range(count - 1)]
        forward.append((count - 1, 0))
        backward = [(target, source) for source, target in forward]
        low = lax.ppermute(
            lax.slice_in_dim(block, block.shape[dim] - width, None, axis=dim), axis, forward
        )
        high = lax.ppermute(lax.slice_in_dim(block, 0, width, axis=dim), axis, backward)
        block = jnp.concatenate([low, block, high], axis=dim)
    return block


def stencil_sum(padded, fields):
    width_x = fields.shape[1]
    width_y = fields.shape[2]
    near = (
        padded[:, 3 : 3 + width_x, 2 : 2 + width_y]
        + padded[:, 1 : 1 + width_x, 2 : 2 + width_y]
        + padded[:, 2 : 2 + width_x, 3 : 3 + width_y]
        + padded[:, 2 : 2 + width_x, 1 : 1 + width_y]
        + jnp.roll(fields, -1, 3)
        + jnp.roll(fields, 1, 3)
    )
    far = (
        padded[:, 4 : 4 + width_x, 2 : 2 + width_y]
        + padded[:, 0:width_x, 2 : 2 + width_y]
        + padded[:, 2 : 2 + width_x, 4 : 4 + width_y]
        + padded[:, 2 : 2 + width_x, 0:width_y]
        + jnp.roll(fields, -2, 3)
        + jnp.roll(fields, 2, 3)
    )
    return 3.0 * center_weight * fields + near_weight * near + far_weight * far


def place_frames(corners, offset_x, offset_y, projectors, width_x, width_y):
    local_x = corners[:, 0] % width_x - offset_x * width_x
    local_y = corners[:, 1] % width_y - offset_y * width_y
    steps_box = jnp.arange(BOX, dtype=jnp.int32)
    pick_x = (
        jnp.arange(width_x, dtype=jnp.int32)[None, None, :]
        == (local_x[:, None] + steps_box[None, :])[:, :, None]
    ).astype(jnp.float32)
    pick_y = (
        jnp.arange(width_y, dtype=jnp.int32)[None, None, :]
        == (local_y[:, None] + steps_box[None, :])[:, :, None]
    ).astype(jnp.float32)
    shapes_table = projectors.reshape(NPROJ, BOX, BOX, BOX)
    frames = jnp.einsum(
        "aix,jilk,aly->ajkxy",
        pick_x,
        shapes_table,
        pick_y,
        precision=highest,
        preferred_element_type=jnp.float32,
    )
    return frames.reshape(corners.shape[0], NPROJ, BOX, width_x * width_y)


def local(orbitals, potential, corners, counts, coupling, projectors, occupations):
    orbital_count = orbitals.shape[1]
    width_x = orbitals.shape[2]
    width_y = orbitals.shape[3]
    width_z = orbitals.shape[4]
    atom_count = corners.shape[0]
    symmetric = 0.5 * (coupling + jnp.swapaxes(coupling, 1, 2))
    active = (jnp.arange(NPROJ, dtype=jnp.int32)[None, :] < counts[:, None]).astype(jnp.float32)
    coupled = symmetric * active[:, :, None] * active[:, None, :]
    corners_x = passed_along(corners, "gx", 1)
    corners_y, corners_xy = passed_along((corners, corners_x), "gy", 1)
    every_corner = jnp.concatenate([corners, corners_x, corners_y, corners_xy], axis=0)
    offset_x = jnp.repeat(jnp.array([0, 1, 0, 1], jnp.int32), atom_count)
    offset_y = jnp.repeat(jnp.array([0, 0, 1, 1], jnp.int32), atom_count)
    frames = place_frames(every_corner, offset_x, offset_y, projectors, width_x, width_y)
    depth_index = (
        (every_corner[:, 2:3] + jnp.arange(BOX, dtype=jnp.int32)[None, :]) % width_z
    ).reshape(-1)
    depth_pick = (depth_index[:, None] == jnp.arange(width_z, dtype=jnp.int32)[None, :]).astype(
        jnp.float32
    )
    fields = orbitals.reshape(2 * orbital_count, width_x, width_y, width_z)
    series = fields
    taylor_term = fields
    for power in range(1, 5):
        padded = padded_2(taylor_term, (("gx", 1), ("gy", 2)), 2)
        laplacian = stencil_sum(padded, taylor_term)
        count_fields = taylor_term.shape[0]
        cells = taylor_term.reshape(count_fields, width_x * width_y, width_z)
        slabs = jnp.einsum(
            "fpz,mz->fpm", cells, depth_pick, precision=highest, preferred_element_type=jnp.float32
        )
        slabs = slabs.reshape(count_fields, width_x * width_y, 4 * atom_count, BOX)
        apply_partial_value = jnp.einsum(
            "fpak,ajkp->ajf", slabs, frames, precision=highest, preferred_element_type=jnp.float32
        )
        own_part, part_x, part_y, part_xy = jnp.split(apply_partial_value, 4, axis=0)
        from_y, from_xy = passed_along((part_y, part_xy), "gy", -1)
        from_x = passed_along(part_x + from_xy, "gx", -1)
        totals = own_part + from_y + from_x
        coefficients = jnp.einsum(
            "aji,aif->ajf", coupled, totals, precision=highest, preferred_element_type=jnp.float32
        )
        coefficients_x = passed_along(coefficients, "gx", 1)
        coefficients_y, coefficients_xy = passed_along((coefficients, coefficients_x), "gy", 1)
        apply_coefficients = jnp.concatenate(
            [coefficients, coefficients_x, coefficients_y, coefficients_xy], axis=0
        )
        values = jnp.einsum(
            "ajf,ajkp->fpak",
            apply_coefficients,
            frames,
            precision=highest,
            preferred_element_type=jnp.float32,
        )
        values = values.reshape(count_fields, width_x * width_y, 4 * atom_count * BOX)
        projected = jnp.einsum(
            "fpm,mz->fpz", values, depth_pick, precision=highest, preferred_element_type=jnp.float32
        ).reshape(taylor_term.shape)
        applied = -0.5 * laplacian + potential[None] * taylor_term + projected
        factor = time_step / power
        taylor_term = jnp.concatenate(
            [factor * applied[orbital_count:], -factor * applied[:orbital_count]], axis=0
        )
        series = series + taylor_term
    propagated = series.reshape(orbitals.shape)
    real_part = propagated[0]
    imag_part = propagated[1]
    partial_density = jnp.sum(
        occupations[:, None, None, None] * (real_part * real_part + imag_part * imag_part), axis=0
    )
    density = lax.psum(partial_density, "band")
    return (propagated, density)


def solution(mesh):
    placed = (
        P(None, "band", "gx", "gy", None),
        P("gx", "gy", None),
        P(("gx", "gy"), None),
        P(("gx", "gy")),
        P(("gx", "gy"), None, None),
        P(),
        P("band"),
    )
    return jax.shard_map(
        local,
        mesh=mesh,
        in_specs=placed,
        out_specs=(P(None, "band", "gx", "gy", None), P("gx", "gy", None)),
        check_vma=False,
    )
```

profile of v0, /device:TPU:1, one launch (start us, length us, event | category | flops | bytes accessed | tf_op | source)
XLA Modules:
  0.0 364.2 jit_solution(6932842483814191955)
XLA Ops:
  8.0 5.5 %collective-permute-start.4 = (s32[4,3]{0,1:T(4,128)S(1)}, s32[4,3]{0,1:T(4,128)S(1)}, u32[]{:S(2)}, u32[]{:S(2)}) collective-permute-start(s32[4,3]{0,1:T(4,128)S(1)} %copy.96), channel_id=1, source_target_pairs={{480,0},{0,32},{32,64},{64,96},{96,128},{128,160},{160,192},{192,2... | collective-permute-start | bytes 152 | tf_op jit(solution)/shard_map/ppermute | solution.py:20
  16.5 3.9 %collective-permute-start.1 = (f32[4,2,16,128]{3,2,1,0:T(8,128)S(1)}, f32[4,2,16,128]{3,2,1,0:T(8,128)S(1)}, u32[]{:S(2)}, u32[]{:S(2)}) collective-permute-start(f32[4,2,16,128]{3,2,1,0:T(8,128)S(1)} %get-tuple-element.73), channel_id=1, source_target_pairs={{0,32},{32,64},{64,96},{96,128},{128,160},{160,192},{192,224},{224... | collective-permute-start | bytes 196616 | tf_op jit(solution)/shard_map/ppermute | solution.py:29
  20.4 8.1 %collective-permute-start = (f32[4,2,16,128]{3,2,1,0:T(8,128)S(1)}, f32[4,2,16,128]{3,2,1,0:T(8,128)S(1)}, u32[]{:S(2)}, u32[]{:S(2)}) collective-permute-start(f32[4,2,16,128]{3,2,1,0:T(8,128)S(1)} %get-tuple-element.72), channel_id=1, source_target_pairs={{32,0},{64,32},{96,64},{128,96},{160,128},{192,160},{224,192},{256... | collective-permute-start | bytes 196616 | tf_op jit(solution)/shard_map/ppermute | solution.py:32
  44.0 6.5 %fusion.8 = f32[16,4,16,16,16]{4,3,2,1,0:T(8,128)} fusion(f32[16,16,4,16,16]{3,1,4,2,0:T(8,128)S(1)} %fusion.96, s32[16,16]{1,0:T(8,128)S(1)} %get-tuple-element.87), kind=kOutput, calls=%fused_computation.8 | convolution fusion | flops 50335744 | bytes 2098176 | tf_op jit(solution)/shard_map/aix,jilk,aly->ajkxy/dot_general | solution.py:72
  50.5 6.2 %reshape.241 = f32[16,4,16,256]{3,2,1,0:T(8,128)S(1)} reshape(f32[16,4,16,16,16]{4,3,2,1,0:T(8,128)} %fusion.8) | data formatting | bytes 2097152 | tf_op jit(solution)/shard_map/reshape | solution.py:80
  57.4 6.1 %convolution_bitcast_fusion.7 = f32[16,4,4]{2,1,0:T(4,128)S(1)} fusion(f32[4,256,16,16]{1,3,2,0:T(8,128)S(1)} %bitcast.143, f32[16,4,16,256]{3,2,1,0:T(8,128)S(1)} %reshape.241), kind=kOutput, calls=%fused_computation.84 | convolution fusion | flops 12582912 | bytes 2098176 | tf_op jit(solution)/shard_map/fpak,ajkp->ajf/dot_general | solution.py:116
  67.1 5.1 %collective-permute-start.9 = (f32[4,4,4]{2,1,0:T(4,128)S(1)}, f32[4,4,4]{2,1,0:T(4,128)S(1)}, u32[]{:S(2)}, u32[]{:S(2)}) collective-permute-start(f32[4,4,4]{2,1,0:T(4,128)S(1)} %slice_add_fusion.26), channel_id=1, source_target_pairs={{32,0},{64,32},{96,64},{128,96},{160,128},{192,160},{224,192},{256... | collective-permute-start | bytes 776 | tf_op jit(solution)/shard_map/ppermute | solution.py:20
  89.2 5.3 %reshape.263 = f32[4,16,16,256]{2,1,0,3:T(8,128)} reshape(f32[4,256,16,16]{1,0,3,2:T(4,128)S(1)} %convolution_bitcast_fusion.3) | data formatting | bytes 2097152 | tf_op jit(solution)/shard_map/fpm,mz->fpz/dot_general | solution.py:139
  95.5 14.6 %fusion.10 = f32[4,16,16,128]{3,2,1,0:T(8,128)S(1)} fusion(f32[4,16,16,256]{2,1,0,3:T(8,128)} %reshape.263, f32[4,2,16,128]{3,2,1,0:T(8,128)S(1)} %collective-permute-done.1, f32[4,16,16,128]{3,2,1,0:T(8,128)S(1)} %bitcast.136, f32[4,2,16,128]{3,2,1,0:T(8,128)S(1)} %collective-permute-done, f32[4,20,18,128]{3,2,1,0:T(8,128)S(1)} %get-tuple-element.15, ...), kind=kOutput, calls=%fused_computation.77 | convolution fusion | flops 406224896 | bytes 6554624 | tf_op jit(solution)/shard_map/fpm,mz->fpz/dot_general | solution.py:139
  113.1 6.3 %convolution_bitcast_fusion.6 = f32[16,4,4]{2,1,0:T(4,128)S(1)} fusion(f32[4,256,16,16]{1,3,2,0:T(8,128)S(1)} %fusion.126, f32[16,4,16,256]{3,2,1,0:T(8,128)S(1)} %reshape.241), kind=kOutput, calls=%fused_computation.83 | convolution fusion | flops 12582912 | bytes 2098176 | tf_op jit(solution)/shard_map/fpak,ajkp->ajf/dot_general | solution.py:116
  125.4 5.1 %collective-permute-start.19 = (f32[4,4,4]{2,1,0:T(4,128)S(1)}, f32[4,4,4]{2,1,0:T(4,128)S(1)}, u32[]{:S(2)}, u32[]{:S(2)}) collective-permute-start(f32[4,4,4]{2,1,0:T(4,128)S(1)} %slice_add_fusion.24), channel_id=1, source_target_pairs={{32,0},{64,32},{96,64},{128,96},{160,128},{192,160},{224,192},{256... | collective-permute-start | bytes 776 | tf_op jit(solution)/shard_map/ppermute | solution.py:20
  133.9 5.9 %collective-permute-done.20 = f32[4,4,4]{2,1,0:T(4,128)S(1)} collective-permute-done((f32[4,4,4]{2,1,0:T(4,128)S(1)}, f32[4,4,4]{2,1,0:T(4,128)S(1)}, u32[]{:S(2)}, u32[]{:S(2)}) %collective-permute-start.20) | collective-permute-done | bytes 288 | tf_op jit(solution)/shard_map/ppermute | solution.py:20
  141.1 5.1 %collective-permute-start.13 = (f32[4,2,16,128]{3,2,1,0:T(8,128)S(1)}, f32[4,2,16,128]{3,2,1,0:T(8,128)S(1)}, u32[]{:S(2)}, u32[]{:S(2)}) collective-permute-start(f32[4,2,16,128]{3,2,1,0:T(8,128)S(1)} %get-tuple-element.61), channel_id=1, source_target_pairs={{32,0},{64,32},{96,64},{128,96},{160,128},{192,160},{224,192},{256... | collective-permute-start | bytes 196616 | tf_op jit(solution)/shard_map/ppermute | solution.py:32
  150.7 4.9 %reshape.264 = f32[4,16,16,256]{2,1,0,3:T(8,128)} reshape(f32[4,256,16,16]{1,0,3,2:T(4,128)S(1)} %convolution_bitcast_fusion.2) | data formatting | bytes 2097152 | tf_op jit(solution)/shard_map/fpm,mz->fpz/dot_general | solution.py:139
  160.4 14.9 %fusion.13 = f32[4,16,16,128]{3,2,1,0:T(8,128)S(1)} fusion(f32[4,16,16,256]{2,1,0,3:T(8,128)} %reshape.264, f32[4,20,18,128]{3,2,1,0:T(8,128)S(1)} %get-tuple-element.11, f32[4,20,18,128]{3,2,1,0:T(8,128)S(1)} %get-tuple-element.10, f32[4,18,16,128]{3,2,1,0:T(8,128)S(1)} %get-tuple-element.59, f32[4,18,16,128]{3,2,1,0:T(8,128)S(1)} %get-tuple-element.58, ...), kind=kOutput, calls=%fused_computation.78 | convolution fusion | flops 405831680 | bytes 8520704 | tf_op jit(solution)/shard_map/fpm,mz->fpz/dot_general | solution.py:139
  178.2 6.5 %convolution_bitcast_fusion.5 = f32[16,4,4]{2,1,0:T(4,128)S(1)} fusion(f32[4,256,16,16]{1,3,2,0:T(8,128)S(1)} %fusion.124, f32[16,4,16,256]{3,2,1,0:T(8,128)S(1)} %reshape.241), kind=kOutput, calls=%fused_computation.82 | convolution fusion | flops 12582912 | bytes 2098176 | tf_op jit(solution)/shard_map/fpak,ajkp->ajf/dot_general | solution.py:116
  184.7 4.3 %collective-permute-start.28 = (f32[4,4,4]{2,1,0:T(4,128)S(1)}, f32[4,4,4]{2,1,0:T(4,128)S(1)}, u32[]{:S(2)}, u32[]{:S(2)}) collective-permute-start(f32[4,4,4]{2,1,0:T(4,128)S(1)} %get-tuple-element.77), channel_id=1, source_target_pairs={{2,0},{4,2},{6,4},{8,6},{10,8},{12,10},{14,12},{16,14},{18,16},{20... | collective-permute-start | bytes 776 | tf_op jit(solution)/shard_map/ppermute | solution.py:20
  190.2 7.0 %collective-permute-start.29 = (f32[4,4,4]{2,1,0:T(4,128)S(1)}, f32[4,4,4]{2,1,0:T(4,128)S(1)}, u32[]{:S(2)}, u32[]{:S(2)}) collective-permute-start(f32[4,4,4]{2,1,0:T(4,128)S(1)} %slice_add_fusion.22), channel_id=1, source_target_pairs={{32,0},{64,32},{96,64},{128,96},{160,128},{192,160},{224,192},{256... | collective-permute-start | bytes 776 | tf_op jit(solution)/shard_map/ppermute | solution.py:20
  202.7 3.8 %collective-permute-done.30 = f32[4,4,4]{2,1,0:T(4,128)S(1)} collective-permute-done((f32[4,4,4]{2,1,0:T(4,128)S(1)}, f32[4,4,4]{2,1,0:T(4,128)S(1)}, u32[]{:S(2)}, u32[]{:S(2)}) %collective-permute-start.30) | collective-permute-done | bytes 288 | tf_op jit(solution)/shard_map/ppermute | solution.py:20
  206.5 3.6 collective-permute-start.32
  210.1 5.1 %collective-permute-start.23 = (f32[4,2,16,128]{3,2,1,0:T(8,128)S(1)}, f32[4,2,16,128]{3,2,1,0:T(8,128)S(1)}, u32[]{:S(2)}, u32[]{:S(2)}) collective-permute-start(f32[4,2,16,128]{3,2,1,0:T(8,128)S(1)} %get-tuple-element.47), channel_id=1, source_target_pairs={{32,0},{64,32},{96,64},{128,96},{160,128},{192,160},{224,192},{256... | collective-permute-start | bytes 196616 | tf_op jit(solution)/shard_map/ppermute | solution.py:32
  217.2 3.5 convolution_bitcast_fusion.1
  220.7 6.3 %reshape.265 = f32[4,16,16,256]{2,1,0,3:T(8,128)} reshape(f32[4,256,16,16]{1,0,3,2:T(4,128)} %convolution_bitcast_fusion.1) | data formatting | bytes 2097152 | tf_op jit(solution)/shard_map/fpm,mz->fpz/dot_general | solution.py:139
  231.2 14.7 %fusion.16 = f32[4,16,16,128]{3,2,1,0:T(8,128)S(1)} fusion(f32[4,16,16,256]{2,1,0,3:T(8,128)} %reshape.265, f32[4,20,18,128]{3,2,1,0:T(8,128)S(1)} %get-tuple-element.7, f32[4,20,18,128]{3,2,1,0:T(8,128)S(1)} %get-tuple-element.6, f32[4,18,16,128]{3,2,1,0:T(8,128)S(1)} %get-tuple-element.45, f32[4,18,16,128]{3,2,1,0:T(8,128)S(1)} %get-tuple-element.44, ...), kind=kOutput, calls=%fused_computation.79 | convolution fusion | flops 405831680 | bytes 8520704 | tf_op jit(solution)/shard_map/fpm,mz->fpz/dot_general | solution.py:139
  249.0 6.3 %convolution_bitcast_fusion.4 = f32[16,4,4]{2,1,0:T(4,128)S(1)} fusion(f32[4,256,16,16]{1,3,2,0:T(8,128)S(1)} %fusion.122, f32[16,4,16,256]{3,2,1,0:T(8,128)S(1)} %reshape.241), kind=kOutput, calls=%fused_computation.81 | convolution fusion | flops 12582912 | bytes 2098176 | tf_op jit(solution)/shard_map/fpak,ajkp->ajf/dot_general | solution.py:116
  259.2 7.0 %collective-permute-start.39 = (f32[4,4,4]{2,1,0:T(4,128)S(1)}, f32[4,4,4]{2,1,0:T(4,128)S(1)}, u32[]{:S(2)}, u32[]{:S(2)}) collective-permute-start(f32[4,4,4]{2,1,0:T(4,128)S(1)} %slice_add_fusion.20), channel_id=1, source_target_pairs={{32,0},{64,32},{96,64},{128,96},{160,128},{192,160},{224,192},{256... | collective-permute-start | bytes 776 | tf_op jit(solution)/shard_map/ppermute | solution.py:20
  271.6 3.9 %collective-permute-done.40 = f32[4,4,4]{2,1,0:T(4,128)S(1)} collective-permute-done((f32[4,4,4]{2,1,0:T(4,128)S(1)}, f32[4,4,4]{2,1,0:T(4,128)S(1)}, u32[]{:S(2)}, u32[]{:S(2)}) %collective-permute-start.40) | collective-permute-done | bytes 288 | tf_op jit(solution)/shard_map/ppermute | solution.py:20
  275.5 3.6 collective-permute-start.42
  279.1 5.1 %collective-permute-start.33 = (f32[4,2,16,128]{3,2,1,0:T(8,128)S(1)}, f32[4,2,16,128]{3,2,1,0:T(8,128)S(1)}, u32[]{:S(2)}, u32[]{:S(2)}) collective-permute-start(f32[4,2,16,128]{3,2,1,0:T(8,128)S(1)} %get-tuple-element.33), channel_id=1, source_target_pairs={{32,0},{64,32},{96,64},{128,96},{160,128},{192,160},{224,192},{256... | collective-permute-start | bytes 196616 | tf_op jit(solution)/shard_map/ppermute | solution.py:32
  289.7 6.1 %reshape.266 = f32[4,16,16,256]{2,1,0,3:T(8,128)} reshape(f32[4,256,16,16]{1,0,3,2:T(4,128)} %convolution_bitcast_fusion) | data formatting | bytes 2097152 | tf_op jit(solution)/shard_map/fpm,mz->fpz/dot_general | solution.py:139
  300.0 15.0 %fusion.19 = f32[4,16,16,128]{3,2,1,0:T(8,128)S(1)} fusion(f32[4,16,16,256]{2,1,0,3:T(8,128)} %reshape.266, f32[4,20,18,128]{3,2,1,0:T(8,128)S(1)} %get-tuple-element.3, f32[4,20,18,128]{3,2,1,0:T(8,128)S(1)} %get-tuple-element.2, f32[4,18,16,128]{3,2,1,0:T(8,128)S(1)} %get-tuple-element.31, f32[4,18,16,128]{3,2,1,0:T(8,128)S(1)} %get-tuple-element.30, ...), kind=kOutput, calls=%fused_computation.80 | convolution fusion | flops 405831680 | bytes 8520704 | tf_op jit(solution)/shard_map/fpm,mz->fpz/dot_general | solution.py:139
  319.0 36.6 %all-reduce.2.cloned.1.call-done = f32[16,16,128]{2,1,0:T(8,128)} async-done(((f32[16,16,128]{2,1,0:T(8,128)}), f32[16,16,128]{2,1,0:T(8,128)}) %all-reduce.2.cloned.1.call-update) | async-done | bytes 131088 | tf_op jit(solution)/shard_map/psum | solution.py:154
  (175 shorter events, 107.2 us)
Async XLA Ops:
  7.2 348.4 %all-reduce.2.cloned.1.call-start = ((), (), s32[]{:S(2)}) async-start(), calls=%async_computation | async-start | bytes 262144 | tf_op jit(solution)/shard_map/psum | solution.py:154
  8.0 31.2 %collective-permute-start.4 = (s32[4,3]{0,1:T(4,128)S(1)}, s32[4,3]{0,1:T(4,128)S(1)}, u32[]{:S(2)}, u32[]{:S(2)}) collective-permute-start(s32[4,3]{0,1:T(4,128)S(1)} %copy.96), channel_id=1, source_target_pairs={{480,0},{0,32},{32,64},{64,96},{96,128},{128,160},{160,192},{192,2... | collective-permute-start | bytes 152 | tf_op jit(solution)/shard_map/ppermute | solution.py:20
  13.5 26.0 %collective-permute-start.5 = (s32[4,3]{0,1:T(4,128)S(1)}, s32[4,3]{0,1:T(4,128)S(1)}, u32[]{:S(2)}, u32[]{:S(2)}) collective-permute-start(s32[4,3]{0,1:T(4,128)S(1)} %copy.96), channel_id=1, source_target_pairs={{30,0},{0,2},{2,4},{4,6},{6,8},{8,10},{10,12},{12,14},{14,16},{16,... | collective-permute-start | bytes 152 | tf_op jit(solution)/shard_map/ppermute | solution.py:20
  16.5 67.7 %collective-permute-start.1 = (f32[4,2,16,128]{3,2,1,0:T(8,128)S(1)}, f32[4,2,16,128]{3,2,1,0:T(8,128)S(1)}, u32[]{:S(2)}, u32[]{:S(2)}) collective-permute-start(f32[4,2,16,128]{3,2,1,0:T(8,128)S(1)} %get-tuple-element.73), channel_id=1, source_target_pairs={{0,32},{32,64},{64,96},{96,128},{128,160},{160,192},{192,224},{224... | collective-permute-start | bytes 196616 | tf_op jit(solution)/shard_map/ppermute | solution.py:29
  20.4 63.8 %collective-permute-start = (f32[4,2,16,128]{3,2,1,0:T(8,128)S(1)}, f32[4,2,16,128]{3,2,1,0:T(8,128)S(1)}, u32[]{:S(2)}, u32[]{:S(2)}) collective-permute-start(f32[4,2,16,128]{3,2,1,0:T(8,128)S(1)} %get-tuple-element.72), channel_id=1, source_target_pairs={{32,0},{64,32},{96,64},{128,96},{160,128},{192,160},{224,192},{256... | collective-permute-start | bytes 196616 | tf_op jit(solution)/shard_map/ppermute | solution.py:32
  65.9 6.3 %collective-permute-start.7 = (f32[4,4,4]{2,1,0:T(4,128)S(1)}, f32[4,4,4]{2,1,0:T(4,128)S(1)}, u32[]{:S(2)}, u32[]{:S(2)}) collective-permute-start(f32[4,4,4]{2,1,0:T(4,128)S(1)} %get-tuple-element.80), channel_id=1, source_target_pairs={{2,0},{4,2},{6,4},{8,6},{10,8},{12,10},{14,12},{16,14},{18,16},{20... | collective-permute-start | bytes 776 | tf_op jit(solution)/shard_map/ppermute | solution.py:20
  73.1 8.4 %collective-permute-start.10 = (f32[4,4,4]{2,1,0:T(4,128)S(1)}, f32[4,4,4]{2,1,0:T(4,128)S(1)}, u32[]{:S(2)}, u32[]{:S(2)}) collective-permute-start(f32[4,4,4]{2,1,0:T(4,128)S(1)} %fusion.179), channel_id=1, source_target_pairs={{480,0},{0,32},{32,64},{64,96},{96,128},{128,160},{160,192},{192,2... | collective-permute-start | bytes 776 | tf_op jit(solution)/shard_map/ppermute | solution.py:20
  76.4 10.3 %collective-permute-start.11 = (f32[4,4,4]{2,1,0:T(4,128)S(1)}, f32[4,4,4]{2,1,0:T(4,128)S(1)}, u32[]{:S(2)}, u32[]{:S(2)}) collective-permute-start(f32[4,4,4]{2,1,0:T(4,128)S(1)} %fusion.179), channel_id=1, source_target_pairs={{30,0},{0,2},{2,4},{4,6},{6,8},{8,10},{10,12},{12,14},{14,16},{16,... | collective-permute-start | bytes 776 | tf_op jit(solution)/shard_map/ppermute | solution.py:20
  84.9 9.5 %collective-permute-start.2 = (f32[4,20,2,128]{3,2,1,0:T(2,128)}, f32[4,20,2,128]{3,2,1,0:T(2,128)S(1)}, u32[]{:S(2)}, u32[]{:S(2)}) collective-permute-start(f32[4,20,2,128]{3,2,1,0:T(2,128)} %get-tuple-element.16), channel_id=1, source_target_pairs={{2,0},{4,2},{6,4},{8,6},{10,8},{12,10},{14,12},{16,14},{18,16},{20... | collective-permute-start | bytes 245768 | tf_op jit(solution)/shard_map/ppermute | solution.py:32
  85.5 8.9 %collective-permute-start.3 = (f32[4,20,2,128]{3,2,1,0:T(2,128)}, f32[4,20,2,128]{3,2,1,0:T(2,128)}, u32[]{:S(2)}, u32[]{:S(2)}) collective-permute-start(f32[4,20,2,128]{3,2,1,0:T(2,128)} %get-tuple-element.17), channel_id=1, source_target_pairs={{0,2},{2,4},{4,6},{6,8},{8,10},{10,12},{12,14},{14,16},{16,18},{18... | collective-permute-start | bytes 245768 | tf_op jit(solution)/shard_map/ppermute | solution.py:29
  119.4 6.0 %collective-permute-start.18 = (f32[4,4,4]{2,1,0:T(4,128)S(1)}, f32[4,4,4]{2,1,0:T(4,128)S(1)}, u32[]{:S(2)}, u32[]{:S(2)}) collective-permute-start(f32[4,4,4]{2,1,0:T(4,128)S(1)} %get-tuple-element.79), channel_id=1, source_target_pairs={{2,0},{4,2},{6,4},{8,6},{10,8},{12,10},{14,12},{16,14},{18,16},{20... | collective-permute-start | bytes 776 | tf_op jit(solution)/shard_map/ppermute | solution.py:20
  123.0 8.7 %collective-permute-start.17 = (f32[4,4,4]{2,1,0:T(4,128)S(1)}, f32[4,4,4]{2,1,0:T(4,128)S(1)}, u32[]{:S(2)}, u32[]{:S(2)}) collective-permute-start(f32[4,4,4]{2,1,0:T(4,128)S(1)} %get-tuple-element.78), channel_id=1, source_target_pairs={{2,0},{4,2},{6,4},{8,6},{10,8},{12,10},{14,12},{16,14},{18,16},{20... | collective-permute-start | bytes 776 | tf_op jit(solution)/shard_map/ppermute | solution.py:20
  125.4 6.3 %collective-permute-start.19 = (f32[4,4,4]{2,1,0:T(4,128)S(1)}, f32[4,4,4]{2,1,0:T(4,128)S(1)}, u32[]{:S(2)}, u32[]{:S(2)}) collective-permute-start(f32[4,4,4]{2,1,0:T(4,128)S(1)} %slice_add_fusion.24), channel_id=1, source_target_pairs={{32,0},{64,32},{96,64},{128,96},{160,128},{192,160},{224,192},{256... | collective-permute-start | bytes 776 | tf_op jit(solution)/shard_map/ppermute | solution.py:20
  131.9 8.0 %collective-permute-start.20 = (f32[4,4,4]{2,1,0:T(4,128)S(1)}, f32[4,4,4]{2,1,0:T(4,128)S(1)}, u32[]{:S(2)}, u32[]{:S(2)}) collective-permute-start(f32[4,4,4]{2,1,0:T(4,128)S(1)} %fusion.176), channel_id=1, source_target_pairs={{480,0},{0,32},{32,64},{64,96},{96,128},{128,160},{160,192},{192,2... | collective-permute-start | bytes 776 | tf_op jit(solution)/shard_map/ppermute | solution.py:20
  133.8 14.4 %collective-permute-start.21 = (f32[4,4,4]{2,1,0:T(4,128)S(1)}, f32[4,4,4]{2,1,0:T(4,128)S(1)}, u32[]{:S(2)}, u32[]{:S(2)}) collective-permute-start(f32[4,4,4]{2,1,0:T(4,128)S(1)} %fusion.176), channel_id=1, source_target_pairs={{30,0},{0,2},{2,4},{4,6},{6,8},{8,10},{10,12},{12,14},{14,16},{16,... | collective-permute-start | bytes 776 | tf_op jit(solution)/shard_map/ppermute | solution.py:20
  139.9 8.3 %collective-permute-start.22 = (f32[4,4,4]{2,1,0:T(4,128)S(1)}, f32[4,4,4]{2,1,0:T(4,128)S(1)}, u32[]{:S(2)}, u32[]{:S(2)}) collective-permute-start(f32[4,4,4]{2,1,0:T(4,128)S(1)} %collective-permute-done.20), channel_id=1, source_target_pairs={{30,0},{0,2},{2,4},{4,6},{6,8},{8,10},{10,12},{12,14},{14,16},{16,... | collective-permute-start | bytes 776 | tf_op jit(solution)/shard_map/ppermute | solution.py:20
  141.1 14.5 %collective-permute-start.13 = (f32[4,2,16,128]{3,2,1,0:T(8,128)S(1)}, f32[4,2,16,128]{3,2,1,0:T(8,128)S(1)}, u32[]{:S(2)}, u32[]{:S(2)}) collective-permute-start(f32[4,2,16,128]{3,2,1,0:T(8,128)S(1)} %get-tuple-element.61), channel_id=1, source_target_pairs={{32,0},{64,32},{96,64},{128,96},{160,128},{192,160},{224,192},{256... | collective-permute-start | bytes 196616 | tf_op jit(solution)/shard_map/ppermute | solution.py:32
  146.3 9.3 %collective-permute-start.14 = (f32[4,2,16,128]{3,2,1,0:T(8,128)S(1)}, f32[4,2,16,128]{3,2,1,0:T(8,128)S(1)}, u32[]{:S(2)}, u32[]{:S(2)}) collective-permute-start(f32[4,2,16,128]{3,2,1,0:T(8,128)S(1)} %get-tuple-element.60), channel_id=1, source_target_pairs={{0,32},{32,64},{64,96},{96,128},{128,160},{160,192},{192,224},{224... | collective-permute-start | bytes 196616 | tf_op jit(solution)/shard_map/ppermute | solution.py:29
  190.2 8.1 %collective-permute-start.27 = (f32[4,4,4]{2,1,0:T(4,128)S(1)}, f32[4,4,4]{2,1,0:T(4,128)S(1)}, u32[]{:S(2)}, u32[]{:S(2)}) collective-permute-start(f32[4,4,4]{2,1,0:T(4,128)S(1)} %get-tuple-element.76), channel_id=1, source_target_pairs={{2,0},{4,2},{6,4},{8,6},{10,8},{12,10},{14,12},{16,14},{18,16},{20... | collective-permute-start | bytes 776 | tf_op jit(solution)/shard_map/ppermute | solution.py:20
  190.2 8.1 %collective-permute-start.29 = (f32[4,4,4]{2,1,0:T(4,128)S(1)}, f32[4,4,4]{2,1,0:T(4,128)S(1)}, u32[]{:S(2)}, u32[]{:S(2)}) collective-permute-start(f32[4,4,4]{2,1,0:T(4,128)S(1)} %slice_add_fusion.22), channel_id=1, source_target_pairs={{32,0},{64,32},{96,64},{128,96},{160,128},{192,160},{224,192},{256... | collective-permute-start | bytes 776 | tf_op jit(solution)/shard_map/ppermute | solution.py:20
  198.5 8.0 %collective-permute-start.30 = (f32[4,4,4]{2,1,0:T(4,128)S(1)}, f32[4,4,4]{2,1,0:T(4,128)S(1)}, u32[]{:S(2)}, u32[]{:S(2)}) collective-permute-start(f32[4,4,4]{2,1,0:T(4,128)S(1)} %fusion.173), channel_id=1, source_target_pairs={{480,0},{0,32},{32,64},{64,96},{96,128},{128,160},{160,192},{192,2... | collective-permute-start | bytes 776 | tf_op jit(solution)/shard_map/ppermute | solution.py:20
  200.4 16.8 %collective-permute-start.31 = (f32[4,4,4]{2,1,0:T(4,128)S(1)}, f32[4,4,4]{2,1,0:T(4,128)S(1)}, u32[]{:S(2)}, u32[]{:S(2)}) collective-permute-start(f32[4,4,4]{2,1,0:T(4,128)S(1)} %fusion.173), channel_id=1, source_target_pairs={{30,0},{0,2},{2,4},{4,6},{6,8},{8,10},{10,12},{12,14},{14,16},{16,... | collective-permute-start | bytes 776 | tf_op jit(solution)/shard_map/ppermute | solution.py:20
  206.5 10.7 %collective-permute-start.32 = (f32[4,4,4]{2,1,0:T(4,128)S(1)}, f32[4,4,4]{2,1,0:T(4,128)S(1)}, u32[]{:S(2)}, u32[]{:S(2)}) collective-permute-start(f32[4,4,4]{2,1,0:T(4,128)S(1)} %collective-permute-done.30), channel_id=1, source_target_pairs={{30,0},{0,2},{2,4},{4,6},{6,8},{8,10},{10,12},{12,14},{14,16},{16,... | collective-permute-start | bytes 776 | tf_op jit(solution)/shard_map/ppermute | solution.py:20
  210.1 16.9 %collective-permute-start.23 = (f32[4,2,16,128]{3,2,1,0:T(8,128)S(1)}, f32[4,2,16,128]{3,2,1,0:T(8,128)S(1)}, u32[]{:S(2)}, u32[]{:S(2)}) collective-permute-start(f32[4,2,16,128]{3,2,1,0:T(8,128)S(1)} %get-tuple-element.47), channel_id=1, source_target_pairs={{32,0},{64,32},{96,64},{128,96},{160,128},{192,160},{224,192},{256... | collective-permute-start | bytes 196616 | tf_op jit(solution)/shard_map/ppermute | solution.py:32
  215.3 11.7 %collective-permute-start.24 = (f32[4,2,16,128]{3,2,1,0:T(8,128)S(1)}, f32[4,2,16,128]{3,2,1,0:T(8,128)S(1)}, u32[]{:S(2)}, u32[]{:S(2)}) collective-permute-start(f32[4,2,16,128]{3,2,1,0:T(8,128)S(1)} %get-tuple-element.46), channel_id=1, source_target_pairs={{0,32},{32,64},{64,96},{96,128},{128,160},{160,192},{192,224},{224... | collective-permute-start | bytes 196616 | tf_op jit(solution)/shard_map/ppermute | solution.py:29
  259.2 8.2 %collective-permute-start.37 = (f32[4,4,4]{2,1,0:T(4,128)S(1)}, f32[4,4,4]{2,1,0:T(4,128)S(1)}, u32[]{:S(2)}, u32[]{:S(2)}) collective-permute-start(f32[4,4,4]{2,1,0:T(4,128)S(1)} %get-tuple-element.74), channel_id=1, source_target_pairs={{2,0},{4,2},{6,4},{8,6},{10,8},{12,10},{14,12},{16,14},{18,16},{20... | collective-permute-start | bytes 776 | tf_op jit(solution)/shard_map/ppermute | solution.py:20
  259.2 8.2 %collective-permute-start.39 = (f32[4,4,4]{2,1,0:T(4,128)S(1)}, f32[4,4,4]{2,1,0:T(4,128)S(1)}, u32[]{:S(2)}, u32[]{:S(2)}) collective-permute-start(f32[4,4,4]{2,1,0:T(4,128)S(1)} %slice_add_fusion.20), channel_id=1, source_target_pairs={{32,0},{64,32},{96,64},{128,96},{160,128},{192,160},{224,192},{256... | collective-permute-start | bytes 776 | tf_op jit(solution)/shard_map/ppermute | solution.py:20
  267.5 8.0 %collective-permute-start.40 = (f32[4,4,4]{2,1,0:T(4,128)S(1)}, f32[4,4,4]{2,1,0:T(4,128)S(1)}, u32[]{:S(2)}, u32[]{:S(2)}) collective-permute-start(f32[4,4,4]{2,1,0:T(4,128)S(1)} %fusion.170), channel_id=1, source_target_pairs={{480,0},{0,32},{32,64},{64,96},{96,128},{128,160},{160,192},{192,2... | collective-permute-start | bytes 776 | tf_op jit(solution)/shard_map/ppermute | solution.py:20
  269.4 16.7 %collective-permute-start.41 = (f32[4,4,4]{2,1,0:T(4,128)S(1)}, f32[4,4,4]{2,1,0:T(4,128)S(1)}, u32[]{:S(2)}, u32[]{:S(2)}) collective-permute-start(f32[4,4,4]{2,1,0:T(4,128)S(1)} %fusion.170), channel_id=1, source_target_pairs={{30,0},{0,2},{2,4},{4,6},{6,8},{8,10},{10,12},{12,14},{14,16},{16,... | collective-permute-start | bytes 776 | tf_op jit(solution)/shard_map/ppermute | solution.py:20
  275.5 10.7 %collective-permute-start.42 = (f32[4,4,4]{2,1,0:T(4,128)S(1)}, f32[4,4,4]{2,1,0:T(4,128)S(1)}, u32[]{:S(2)}, u32[]{:S(2)}) collective-permute-start(f32[4,4,4]{2,1,0:T(4,128)S(1)} %collective-permute-done.40), channel_id=1, source_target_pairs={{30,0},{0,2},{2,4},{4,6},{6,8},{8,10},{10,12},{12,14},{14,16},{16,... | collective-permute-start | bytes 776 | tf_op jit(solution)/shard_map/ppermute | solution.py:20
  279.1 16.7 %collective-permute-start.33 = (f32[4,2,16,128]{3,2,1,0:T(8,128)S(1)}, f32[4,2,16,128]{3,2,1,0:T(8,128)S(1)}, u32[]{:S(2)}, u32[]{:S(2)}) collective-permute-start(f32[4,2,16,128]{3,2,1,0:T(8,128)S(1)} %get-tuple-element.33), channel_id=1, source_target_pairs={{32,0},{64,32},{96,64},{128,96},{160,128},{192,160},{224,192},{256... | collective-permute-start | bytes 196616 | tf_op jit(solution)/shard_map/ppermute | solution.py:32
  284.3 11.6 %collective-permute-start.34 = (f32[4,2,16,128]{3,2,1,0:T(8,128)S(1)}, f32[4,2,16,128]{3,2,1,0:T(8,128)S(1)}, u32[]{:S(2)}, u32[]{:S(2)}) collective-permute-start(f32[4,2,16,128]{3,2,1,0:T(8,128)S(1)} %get-tuple-element.32), channel_id=1, source_target_pairs={{0,32},{32,64},{64,96},{96,128},{128,160},{160,192},{192,224},{224... | collective-permute-start | bytes 196616 | tf_op jit(solution)/shard_map/ppermute | solution.py:29
  (24 other events, 217.4 us)
Sparse Core Ops, SparseCore 0:
  316.9 38.6 all-reduce.1
where the time goes:
time: 369 us; the launch traced here: 364 us
  starting transfers between devices  112 us (30%)
  matrix products  109 us (30%)
  waiting for transfers between devices  63.2 us (17%)
  local copies, waits for them, and re-layouts  43.2 us (12%)
  other arithmetic  21.8 us (6%)
  between operations  14.9 us (4%)
    ppermute x27, starting transfers between devices, passed_along(): return lax.ppermute(block, axis, route)  71.4 us
    dot_general x4, matrix products, local(): jnp.einsum('fpm,mz->fpz', values, depth_pick, precision=highest, preferre...  59.1 us
    psum x1, waiting for transfers between devices, local(): density = lax.psum(partial_density, 'band')  36.6 us
    ppermute x8, starting transfers between devices, padded_2(): lax.ppermute(lax.slice_in_dim(block, 0, width, axis=dim), axis, backward)  25.7 us
    dot_general x4, matrix products, local(): jnp.einsum('fpak,ajkp->ajf', slabs, frames, precision=highest, preferred_...  25.3 us
    dot_general x4, local copies, waits for them, and re-layouts, local(): jnp.einsum('fpm,mz->fpz', values, depth_pick, precision=highest, preferre...  22.5 us
    ppermute x27, waiting for transfers between devices, passed_along(): return lax.ppermute(block, axis, route)  19.8 us
    ppermute x8, starting transfers between devices, padded_2(): lax.ppermute(lax.slice_in_dim(block, block.shape[dim] - width, None, axis...  14.5 us
  transfers between devices with their start and end apart: 44, of which 12 were waited for; matrix products, arithmetic and copies ran while one was open for 22% of the time, Pallas kernels for 0%

commit v1 on v0

v1 whole, which is shorter than its diff:
```python
import jax
import jax.numpy as jnp
from jax import lax
from jax.experimental import pallas as pl
from jax.experimental.pallas import tpu as pltpu
from jax.sharding import PartitionSpec as P

BOX = 16
NPROJ = 4
CELL = 16
LANES = 128
FIELDS = 4
STEPS = 4
TIME_STEP = 0.12
MESH = pl.DeviceIdType.MESH
f32 = jnp.float32
bf16 = jnp.bfloat16

NEAR = tuple((dx, dy) for dx in (-1, 1, 0) for dy in (-1, 1, 0) if (dx, dy) != (0, 0))
ABOVE = ((1, 1), (1, 0), (0, 1))
SIDES = ((1, 0), (-1, 0), (0, 1), (0, -1))


def peer(step_x, step_y):
    size_x, size_y = lax.axis_size("gx"), lax.axis_size("gy")
    return (
        lax.rem(lax.axis_index("gx") + step_x + size_x, size_x),
        lax.rem(lax.axis_index("gy") + step_y + size_y, size_y),
        lax.axis_index("band"),
    )


def partner():
    return (lax.axis_index("gx"), lax.axis_index("gy"), 1 - lax.axis_index("band"))


def lane_index(shape):
    return lax.broadcasted_iota(jnp.int32, shape, len(shape) - 1)


def row_index(shape):
    return lax.broadcasted_iota(jnp.int32, shape, len(shape) - 2)


def halves(x):
    high = x.astype(bf16)
    low = (x - high.astype(f32)).astype(bf16)
    return high, low


def thirds(x):
    high = x.astype(bf16)
    rest = x - high.astype(f32)
    mid = rest.astype(bf16)
    low = (rest - mid.astype(f32)).astype(bf16)
    return high, mid, low


def dot_exact(x, pick):
    rows = x.shape[0]
    r = jnp.dot(jnp.concatenate(thirds(x), axis=0), pick, preferred_element_type=f32)
    return r[:rows] + r[rows : 2 * rows] + r[2 * rows :]


def kernel(
    fields_ref, potential_ref, info_ref, projectors_ref, occupations_ref,
    propagated_ref, density_ref,
    term, side_y, local_part, series, pot, info_in, boxes, placed_y, frames,
    pick_in, pick_out, compact, expand, coupled, coef, split_term, slabs, split_values,
    shares, shares_out, shares_in, dens, dens_in, result,
    load_sem, info_send, info_recv, side_send, side_recv, share_send, share_recv,
    dens_send, dens_recv, store_sem,
):
    inner = pl.ds(2, CELL)

    barrier = pltpu.get_barrier_semaphore()
    for d in NEAR:
        pl.semaphore_signal(barrier, inc=1, device_id=peer(*d), device_id_type=MESH)
    pl.semaphore_signal(barrier, inc=1, device_id=partner(), device_id_type=MESH)

    load_fields = [
        pltpu.make_async_copy(fields_ref.at[f], term.at[0, f, inner], load_sem.at[f])
        for f in range(FIELDS)
    ]
    load_potential = pltpu.make_async_copy(potential_ref, pot, load_sem.at[FIELDS])
    for copy in load_fields:
        copy.start()
    load_potential.start()

    r = row_index((2 * LANES, LANES))
    l = lane_index((2 * LANES, LANES))
    compact[...] = jnp.where((l < 64) & (l % 16 == r // 16), 1.0, 0.0).astype(bf16)
    r = row_index((LANES, 2 * LANES))
    l = lane_index((LANES, 2 * LANES))
    expand[...] = jnp.where(r % 16 == l // 16, 1.0, 0.0).astype(bf16)
    fold = jnp.where(
        row_index((LANES, LANES)) % 16 == lane_index((LANES, LANES)) % 16, 1.0, 0.0
    ).astype(bf16)

    own_group = row_index((8, LANES)) == lane_index((8, LANES)) // 16
    for j in range(NPROJ):
        pieces = []
        for c in range(2 * BOX):
            line = projectors_ref[j : j + 1, c * LANES : (c + 1) * LANES]
            pieces.append(jnp.where(own_group, jnp.broadcast_to(line, (8, LANES)), 0.0))
        boxes[j] = dot_exact(jnp.concatenate(pieces, axis=0), fold).reshape(BOX, BOX, LANES)

    pl.semaphore_wait(barrier, len(NEAR) + 1)

    info_copies = [
        pltpu.make_async_remote_copy(
            src_ref=info_ref, dst_ref=info_in.at[i], send_sem=info_send.at[i],
            recv_sem=info_recv.at[i], device_id=peer(*d), device_id_type=MESH,
        )
        for i, d in enumerate(ABOVE)
    ]
    for copy in info_copies:
        copy.start()

    def side_copies(n):
        copies = []
        for k, d in enumerate(SIDES):
            if k == 0:
                src, dst = term.at[n, :, pl.ds(CELL, 2)], term.at[n, :, pl.ds(0, 2)]
            elif k == 1:
                src, dst = term.at[n, :, pl.ds(2, 2)], term.at[n, :, pl.ds(CELL + 2, 2)]
            else:
                rows = pl.ds(CELL - 2, 2) if k == 2 else pl.ds(0, 2)
                src, dst = term.at[n, :, inner, rows], side_y.at[n, :, :, rows]
            copies.append(
                pltpu.make_async_remote_copy(
                    src_ref=src, dst_ref=dst, send_sem=side_send.at[n, k],
                    recv_sem=side_recv.at[n, k], device_id=peer(*d), device_id_type=MESH,
                )
            )
        return copies

    def share_copies(n):
        return [
            pltpu.make_async_remote_copy(
                src_ref=shares_out.at[n, k], dst_ref=shares_in.at[n, k],
                send_sem=share_send.at[n, k], recv_sem=share_recv.at[n, k],
                device_id=peer(*d), device_id_type=MESH,
            )
            for k, d in enumerate(NEAR)
        ]

    for copy in load_fields:
        copy.wait()
    for copy in side_copies(0):
        copy.start()

    def split_first(x, _):
        for f in range(FIELDS):
            high, low = halves(term[0, f, x + 2])
            split_term[f, x, :, :LANES] = high
            split_term[f, x, :, LANES:] = low
        return 0

    lax.fori_loop(0, CELL, split_first, 0)
    load_potential.wait()

    for copy in info_copies:
        copy.wait_recv()

    lane = lane_index((1, LANES))
    upper = lane >= 64
    from_xy, from_x, from_y = (info_in.at[i] for i in range(3))
    near_x = []
    for h in range(2):
        a, b = (info_ref, from_x) if h == 0 else (from_y, from_xy)
        near_x.append(jnp.where(upper, b[...], a[...]))
    for h in range(2):
        depth = (near_x[h][2:3].astype(jnp.int32) + lane % 16) % LANES
        hit = row_index((LANES, LANES)) == depth
        pick = jnp.where(hit, 1.0, 0.0).astype(bf16)
        pick_in[:LANES, h * LANES : (h + 1) * LANES] = pick
        pick_in[LANES:, h * LANES : (h + 1) * LANES] = pick
        pick_out[:, h * LANES : (h + 1) * LANES] = pick
        pick_out[:, (h + 2) * LANES : (h + 3) * LANES] = pick
        for i in range(NPROJ):
            rows = near_x[h][8 + 4 * i : 12 + 4 * i]
            coupled[i, :, h * LANES : (h + 1) * LANES] = jnp.concatenate([rows] * FIELDS, axis=0)

    row = row_index((CELL, LANES))
    for h in range(2):
        at_y = near_x[h][1:2].astype(jnp.int32)
        shift = jnp.broadcast_to(at_y if h == 0 else CELL - at_y, (CELL, LANES))
        bits = []
        for b in range(4):
            step = 1 << b
            stays = row >= step if h == 0 else row < CELL - step
            moved = (shift // step) % 2 == 1
            bits.append((step if h == 0 else CELL - step, moved & stays, moved & ~stays))
        whole = shift >= CELL

        def place_y(i, _, bits=bits, whole=whole, h=h):
            for j in range(NPROJ):
                v = boxes[j, i]
                for step, keep, drop in bits:
                    rolled = pltpu.roll(v, step, 0)
                    v = jnp.where(keep, rolled, jnp.where(drop, 0.0, v))
                placed_y[h, j, i] = jnp.where(whole, 0.0, v)
            return 0

        lax.fori_loop(0, BOX, place_y, 0)

    for h in range(2):
        at_x = jnp.broadcast_to(near_x[h][0:1].astype(jnp.int32), (CELL, LANES))
        above = jnp.broadcast_to(upper, (CELL, LANES))
        down = [~above & ((at_x // (1 << b)) % 2 == 1) for b in range(4)]
        up = [above & (((CELL - at_x) // (1 << b)) % 2 == 1) for b in range(4)]
        whole = above & (at_x == 0)

        def place_x(j, _, down=down, up=up, whole=whole, h=h):
            v = [placed_y[h, j, i] for i in range(BOX)]
            zero = jnp.zeros((CELL, LANES), f32)
            for b in range(4):
                step = 1 << b
                v = [
                    jnp.where(
                        down[b],
                        v[x - step] if x >= step else zero,
                        jnp.where(up[b], v[x + step] if x + step < CELL else zero, v[x]),
                    )
                    for x in range(CELL)
                ]
            for x in range(CELL):
                frames[h, j, x] = jnp.where(whole, 0.0, v[x])
            return 0

        lax.fori_loop(0, NPROJ, place_x, 0)

    def send_shares(n):
        def slab(f, _):
            cells = split_term[f].reshape(CELL * CELL, 2 * LANES)
            slabs[f] = jnp.dot(cells, pick_in[...], preferred_element_type=f32).reshape(
                CELL, CELL, 2 * LANES
            )
            return 0

        lax.fori_loop(0, FIELDS, slab, 0)
        sums = []
        for h in range(2):

            def add(x, totals, h=h):
                frame = [frames[h, j, x] for j in range(NPROJ)]
                new = []
                for f in range(FIELDS):
                    part = slabs[f, x, :, h * LANES : (h + 1) * LANES]
                    for j in range(NPROJ):
                        product = part * frame[j]
                        new.append(totals[f * NPROJ + j] + product[:8] + product[8:])
                return tuple(new)

            zero = jnp.zeros((8, LANES), f32)
            totals = lax.fori_loop(0, CELL, add, (zero,) * (FIELDS * NPROJ))
            sums.append(jnp.concatenate([jnp.sum(t, axis=0, keepdims=True) for t in totals], axis=0))
        lines = dot_exact(jnp.concatenate(sums, axis=1), compact[...])
        mine = jnp.zeros((NPROJ, LANES), f32)
        lane4 = lane_index((NPROJ, LANES))
        for f in range(FIELDS):
            mine = mine + jnp.where(lane4 // 16 == f, lines[4 * f : 4 * f + 4], 0.0)
        shares[...] = mine
        slot = (lane4 // 4) % 4
        valid = lane4 < 64
        for k, (dx, dy) in enumerate(NEAR):
            keep = valid
            if dx:
                keep = keep & (slot % 2 == (1 if dx == 1 else 0))
            if dy:
                keep = keep & (slot // 2 == (1 if dy == 1 else 0))
            moved = pltpu.roll(mine, (4 * dx + 8 * dy) % LANES, 1)
            shares_out[n, k] = jnp.where(keep, moved, 0.0)
        for copy in share_copies(n):
            copy.start()

    send_shares(0)

    row16 = row_index((CELL, LANES))

    def make_term(n, store):
        last = n - 1
        for copy in side_copies(last):
            copy.wait_recv()

        def stencil(x, _):
            v = pot[x]
            for f in range(FIELDS):
                u = term[last, f, x + 2]
                edge = side_y[last, f, x]
                near = term[last, f, x + 1] + term[last, f, x + 3]
                far = term[last, f, x] + term[last, f, x + 4]
                near = near + pltpu.roll(jnp.where(row16 == 0, edge, u), CELL - 1, 0)
                near = near + pltpu.roll(jnp.where(row16 == CELL - 1, edge, u), 1, 0)
                far = far + pltpu.roll(jnp.where(row16 < 2, edge, u), CELL - 2, 0)
                far = far + pltpu.roll(jnp.where(row16 >= CELL - 2, edge, u), 2, 0)
                near = near + pltpu.roll(u, 1, 1) + pltpu.roll(u, LANES - 1, 1)
                far = far + pltpu.roll(u, 2, 1) + pltpu.roll(u, LANES - 2, 1)
                local_part[f, x] = (v + 3.75) * u + (-2.0 / 3.0) * near + (1.0 / 24.0) * far
            return 0

        lax.fori_loop(0, CELL, stencil, 0)

        for copy in share_copies(last):
            copy.wait_recv()
        total = shares[...]
        for k in range(len(NEAR)):
            total = total + shares_in[last, k]
        field_of_row = row_index((FIELDS * NPROJ, LANES)) // NPROJ
        field_of_lane = lane_index((FIELDS * NPROJ, LANES)) // 16
        lines = [
            jnp.where(
                field_of_row == field_of_lane,
                jnp.broadcast_to(total[i : i + 1], (FIELDS * NPROJ, LANES)),
                0.0,
            )
            for i in range(NPROJ)
        ]
        wide = dot_exact(jnp.concatenate(lines, axis=0), expand[...])
        rows = FIELDS * NPROJ
        weights = coupled[0] * wide[:rows]
        for i in range(1, NPROJ):
            weights = weights + coupled[i] * wide[i * rows : (i + 1) * rows]
        coef[...] = weights

        for h in range(2):
            lanes = pl.ds(h * LANES, LANES)

            def spread(x, _, h=h, lanes=lanes):
                frame = [frames[h, j, x] for j in range(NPROJ)]
                for f in range(FIELDS):
                    value = coef[f * NPROJ : f * NPROJ + 1, lanes] * frame[0]
                    for j in range(1, NPROJ):
                        value = value + coef[f * NPROJ + j : f * NPROJ + j + 1, lanes] * frame[j]
                    high, low = halves(value)
                    split_values[f, x, :, h * LANES : (h + 1) * LANES] = high
                    split_values[f, x, :, (h + 2) * LANES : (h + 3) * LANES] = low
                return 0

            lax.fori_loop(0, CELL, spread, 0)

        factor = TIME_STEP / (jnp.zeros((CELL, LANES), f32) + n)
        for f in range(FIELDS):
            source = (f + 2) % 4
            projected = lax.dot_general(
                split_values[source].reshape(CELL * CELL, 4 * LANES), pick_out[...],
                (((1,), (1,)), ((), ())), preferred_element_type=f32,
            )
            signed = factor if f < 2 else -factor
            local_part[source] = local_part[source] + projected.reshape(CELL, CELL, LANES)
            store(f, source, signed)

    def step(n, _):
        def store(f, source, signed):
            def line(x, _):
                value = signed * local_part[source, x]
                term[n, f, x + 2] = value
                high, low = halves(value)
                split_term[f, x, :, :LANES] = high
                split_term[f, x, :, LANES:] = low
                return 0

            lax.fori_loop(0, CELL, line, 0)

        make_term(n, store)
        for copy in side_copies(n):
            copy.start()
        send_shares(n)
        return 0

    lax.fori_loop(1, STEPS, step, 0)

    def store_last(f, source, signed):
        def line(x, _):
            total = term[0, f, x + 2] + term[1, f, x + 2]
            total = total + term[2, f, x + 2] + term[3, f, x + 2]
            result[f, x] = total + signed * local_part[source, x]
            return 0

        lax.fori_loop(0, CELL, line, 0)

    make_term(STEPS, store_last)

    def density(x, _):
        total = jnp.zeros((CELL, LANES), f32)
        for f in range(FIELDS):
            total = total + occupations_ref[f % 2 : f % 2 + 1, :] * (result[f, x] * result[f, x])
        dens[x] = total
        return 0

    lax.fori_loop(0, CELL, density, 0)
    send = pltpu.make_async_remote_copy(
        src_ref=dens, dst_ref=dens_in, send_sem=dens_send, recv_sem=dens_recv,
        device_id=partner(), device_id_type=MESH,
    )
    send.start()
    store_result = pltpu.make_async_copy(result, propagated_ref, store_sem)
    store_result.start()
    for copy in info_copies:
        copy.wait_send()

    def drain(n, _):
        for copy in side_copies(n) + share_copies(n):
            copy.wait_send()
        return 0

    lax.fori_loop(0, STEPS, drain, 0)
    send.wait_recv()

    density_ref[...] = dens[...] + dens_in[...]
    send.wait_send()
    store_result.wait()


def atom_lines(corners, counts, coupling):
    symmetric = 0.5 * (coupling + jnp.swapaxes(coupling, 1, 2))
    active = (jnp.arange(NPROJ, dtype=jnp.int32)[None, :] < counts[:, None]).astype(f32)
    coupled = symmetric * active[:, :, None] * active[:, None, :]
    corner = jnp.concatenate([corners[:, :2] % CELL, corners[:, 2:]], axis=1).astype(f32)
    columns = jnp.swapaxes(coupled, 1, 2).reshape(-1, NPROJ * NPROJ)
    rows = jnp.concatenate([corner, jnp.zeros((corner.shape[0], 5), f32), columns], axis=1)
    return jnp.tile(jnp.repeat(rows.T, BOX, axis=1), (1, 2))


def local(orbitals, potential, corners, counts, coupling, projectors, occupations):
    fields = orbitals.reshape(FIELDS, CELL, CELL, LANES)
    info = atom_lines(corners, counts, coupling)
    weights = jnp.broadcast_to(occupations[:, None], (2, LANES))
    vmem = pl.BlockSpec(memory_space=pltpu.VMEM)
    hbm = pl.BlockSpec(memory_space=pl.ANY)
    grid = (CELL, CELL, LANES)
    dma = pltpu.SemaphoreType.DMA
    propagated, density = pl.pallas_call(
        kernel,
        out_shape=(
            jax.ShapeDtypeStruct((FIELDS,) + grid, f32),
            jax.ShapeDtypeStruct(grid, f32),
        ),
        in_specs=[hbm, hbm, vmem, vmem, vmem],
        out_specs=(hbm, vmem),
        scratch_shapes=[
            pltpu.VMEM((STEPS, FIELDS, CELL + 4, CELL, LANES), f32),
            pltpu.VMEM((STEPS, FIELDS) + grid, f32),
            pltpu.VMEM((FIELDS,) + grid, f32),
            pltpu.VMEM((8, LANES), f32),
            pltpu.VMEM(grid, f32),
            pltpu.VMEM((3, 24, LANES), f32),
            pltpu.VMEM((NPROJ,) + grid, f32),
            pltpu.VMEM((2, NPROJ) + grid, f32),
            pltpu.VMEM((2, NPROJ) + grid, f32),
            pltpu.VMEM((2 * LANES, 2 * LANES), bf16),
            pltpu.VMEM((LANES, 4 * LANES), bf16),
            pltpu.VMEM((2 * LANES, LANES), bf16),
            pltpu.VMEM((LANES, 2 * LANES), bf16),
            pltpu.VMEM((NPROJ, FIELDS * NPROJ, 2 * LANES), f32),
            pltpu.VMEM((FIELDS * NPROJ, 2 * LANES), f32),
            pltpu.VMEM((FIELDS, CELL, CELL, 2 * LANES), bf16),
            pltpu.VMEM((FIELDS, CELL, CELL, 2 * LANES), f32),
            pltpu.VMEM((FIELDS, CELL, CELL, 4 * LANES), bf16),
            pltpu.VMEM((NPROJ, LANES), f32),
            pltpu.VMEM((STEPS, len(NEAR), NPROJ, LANES), f32),
            pltpu.VMEM((STEPS, len(NEAR), NPROJ, LANES), f32),
            pltpu.VMEM(grid, f32),
            pltpu.VMEM(grid, f32),
            pltpu.VMEM((FIELDS,) + grid, f32),
            dma((FIELDS + 1,)),
            dma((3,)),
            dma((3,)),
            dma((STEPS, 4)),
            dma((STEPS, 4)),
            dma((STEPS, len(NEAR))),
            dma((STEPS, len(NEAR))),
            dma,
            dma,
            dma,
        ],
        compiler_params=pltpu.CompilerParams(
            collective_id=1, has_side_effects=True, vmem_limit_bytes=48 * 2**20
        ),
    )(fields, potential, info, projectors, weights)
    return propagated.reshape(orbitals.shape), density


def solution(mesh):
    placed = (
        P(None, "band", "gx", "gy", None),
        P("gx", "gy", None),
        P(("gx", "gy"), None),
        P(("gx", "gy")),
        P(("gx", "gy"), None, None),
        P(),
        P("band"),
    )
    return jax.shard_map(
        local,
        mesh=mesh,
        in_specs=placed,
        out_specs=(P(None, "band", "gx", "gy", None), P("gx", "gy", None)),
        check_vma=False,
    )
```

time: 369 us -> 70.3 us (0.19)
  the two profiles are of different devices: /device:TPU:1 before, /device:TPU:25 now
where the time goes in v1:
time: 70.3 us; the launch traced here: 69.6 us
  Pallas kernels  59.9 us (85%)
  local copies, waits for them, and re-layouts  5.88 us (8%)
  other arithmetic  3.06 us (4%)
    pallas_call x1, Pallas kernels, local(): pl.pallas_call(kernel, out_shape=(jax.ShapeDtypeStruct((FIELDS,) + grid,...  59.9 us
    unnamed x9, local copies, waits for them, and re-layouts  3.96 us

profile of v1, /device:TPU:25, one launch (start us, length us, event | category | flops | bytes accessed | tf_op | source)
XLA Modules:
  0.0 69.6 jit_solution(4755613325346081173)
XLA Ops:
  0.6 0.0 copy-start.1
  0.6 0.1 pad.1.clone
  0.7 0.7 %broadcast_in_dim.5.occupations_ref = f32[2,128]{1,0:T(2,128)S(1)} broadcast(f32[2]{0:T(128)} %param.13), dimensions={0} | broadcast | bytes 1032 | tf_op jit(solution)/shard_map/broadcast_in_dim | solution.py:429
  1.4 0.8 %slice.7 = s32[4,1]{1,0:T(4,128)S(1)} slice(s32[4,3]{1,0:T(4,128)} %param.9), slice={[0:4], [2:3]} | slice | bytes 32 | tf_op jit(solution)/shard_map/slice | solution.py:420
  2.2 0.7 add_select_fusion
  2.9 0.1 add_convert_fusion
  3.0 0.7 %fusion.4 = f32[4,4]{1,0:T(4,128)S(1)} fusion(s32[4]{0:T(128)} %param.10), kind=kLoop, calls=%fused_computation.11 | loop fusion | flops 32 | bytes 80 | tf_op jit(solution)/shard_map/convert_element_type | solution.py:418
  3.7 0.7 %fusion.5 = f32[4,4]{1,0:T(4,128)S(1)} fusion(s32[4]{0:T(128)} %param.10), kind=kLoop, calls=%fused_computation.12 | loop fusion | flops 32 | bytes 80 | tf_op jit(solution)/shard_map/mul | solution.py:419
  4.4 0.8 %copy.12 = f32[4,4,4]{1,2,0:T(4,128)S(1)} copy(f32[4,4,4]{2,1,0:T(4,128)} %param.11) | data formatting | bytes 512 | tf_op args[4]
  5.2 0.8 %fusion.2 = f32[4,4,4]{1,2,0:T(4,128)S(1)} fusion(f32[4,4,4]{2,1,0:T(4,128)} %param.11, f32[4,4,4]{1,2,0:T(4,128)S(1)} %copy.12, f32[4,4]{1,0:T(4,128)S(1)} %fusion.4, f32[4,4]{1,0:T(4,128)S(1)} %fusion.5), kind=kLoop, calls=%fused_computation.3 | loop fusion | flops 192 | bytes 896 | tf_op jit(solution)/shard_map/transpose | solution.py:421
  6.0 0.1 copy.13
  6.1 0.1 reshape.57
  6.2 0.1 maximum_bitcast_fusion
  6.3 0.0 copy-start.2
  6.3 0.1 copy.14
  6.4 0.1 tile.12.info_ref
  6.4 0.0 copy-done.1
  6.5 0.7 copy-done.2
  7.1 0.0 copy-start
  7.1 1.0 %copy-done = f32[2,2,16,16,128]{4,3,2,1,0:T(8,128)S(1)} copy-done((f32[2,2,16,16,128]{4,3,2,1,0:T(8,128)S(1)}, f32[2,2,16,16,128]{4,3,2,1,0:T(8,128)}, u32[]{:S(2)}) %copy-start) | copy-done | bytes 524312
  8.2 59.9 %shard_map.86 = (f32[4,16,16,128]{3,2,1,0:T(8,128)S(1)}, f32[16,16,128]{2,1,0:T(8,128)S(1)}) custom-call(f32[4,16,16,128]{3,2,1,0:T(8,128)S(1)} %bitcast.15, f32[16,16,128]{2,1,0:T(8,128)S(1)} %copy-done.1, f32[24,128]{1,0:T(8,128)S(1)} %tile.12.info_ref, f32[4,4096]{1,0:T(4,128)S(1)} %copy-done.2, f32[2,128]{1,0:T(2,128)S(1)} %broadcast_in_dim.5.occupations_ref), custom_call_target="tpu_custom_call" | custom-call | tf_op jit(solution)/shard_map/pallas_call | solution.py:434
  68.1 0.8 %copy.17 = f32[2,2,16,16,128]{4,3,2,1,0:T(8,128)} copy(f32[2,2,16,16,128]{4,3,2,1,0:T(8,128)S(1)} %bitcast.16) | data formatting | bytes 1048576
  68.9 0.7 copy.18
  (3 shorter events, 0.0 us)
Async XLA Ops:
  0.6 5.8 %copy-start.1 = (f32[16,16,128]{2,1,0:T(8,128)S(1)}, f32[16,16,128]{2,1,0:T(8,128)}, u32[]{:S(2)}) copy-start(f32[16,16,128]{2,1,0:T(8,128)} %potential_ref.1) | copy-start | bytes 393220
  6.3 0.8 %copy-start.2 = (f32[4,4096]{1,0:T(4,128)S(1)}, f32[4,4096]{1,0:T(4,128)}, u32[]{:S(2)}) copy-start(f32[4,4096]{1,0:T(4,128)} %projectors_ref.1) | copy-start | bytes 196612
  7.1 1.0 %copy-start = (f32[2,2,16,16,128]{4,3,2,1,0:T(8,128)S(1)}, f32[2,2,16,16,128]{4,3,2,1,0:T(8,128)}, u32[]{:S(2)}) copy-start(f32[2,2,16,16,128]{4,3,2,1,0:T(8,128)} %param.7) | copy-start | bytes 1572868

commit v2 on v1

v2 whole, which is shorter than its diff:
```python
import jax
import jax.numpy as jnp
from jax import lax
from jax.experimental import pallas as pl
from jax.experimental.pallas import tpu as pltpu
from jax.sharding import PartitionSpec as P

BOX = 16
NPROJ = 4
CELL = 16
LANES = 128
FIELDS = 4
STEPS = 4
PAIR = 2
UNROLL = 4
VMEM_BYTES = 60 * 2**20
TIME_STEP = 0.12
MESH = pl.DeviceIdType.MESH
f32 = jnp.float32
bf16 = jnp.bfloat16

NEAR = tuple((dx, dy) for dx in (-1, 1, 0) for dy in (-1, 1, 0) if (dx, dy) != (0, 0))
ABOVE = ((1, 1), (1, 0), (0, 1))
SIDES = ((1, 0), (-1, 0), (0, 1), (0, -1))


def peer(step_x, step_y):
    size_x, size_y = lax.axis_size("gx"), lax.axis_size("gy")
    return (
        lax.rem(lax.axis_index("gx") + step_x + size_x, size_x),
        lax.rem(lax.axis_index("gy") + step_y + size_y, size_y),
        lax.axis_index("band"),
    )


def partner():
    return (lax.axis_index("gx"), lax.axis_index("gy"), 1 - lax.axis_index("band"))


def lane_index(shape):
    return lax.broadcasted_iota(jnp.int32, shape, len(shape) - 1)


def row_index(shape):
    return lax.broadcasted_iota(jnp.int32, shape, len(shape) - 2)


def halves(x):
    high = x.astype(bf16)
    low = (x - high.astype(f32)).astype(bf16)
    return high, low


def thirds(x):
    high = x.astype(bf16)
    rest = x - high.astype(f32)
    mid = rest.astype(bf16)
    low = (rest - mid.astype(f32)).astype(bf16)
    return high, mid, low


def dot_exact(x, pick):
    rows = x.shape[0]
    r = jnp.dot(jnp.concatenate(thirds(x), axis=0), pick, preferred_element_type=f32)
    return r[:rows] + r[rows : 2 * rows] + r[2 * rows :]


def kernel(
    fields_ref, potential_ref, corners_hbm, counts_hbm, coupling_hbm, projectors_ref, occupations_hbm,
    propagated_ref, density_ref,
    term, side_y, local_part, pot, table, corners_ref, counts_ref, coupling_ref, occupations_ref, info, info_in, boxes, placed_y, frames,
    pick_in, pick_out, compact, expand, coupled, coef, split_term, slabs, split_values, projected,
    shares, shares_out, shares_in, dens, dens_in,
    load_sem, info_send, info_recv, side_send, side_recv, share_send, share_recv,
    dens_send, dens_recv,
):
    inner = pl.ds(2, CELL)

    barrier = pltpu.get_barrier_semaphore()
    for d in NEAR:
        pl.semaphore_signal(barrier, inc=1, device_id=peer(*d), device_id_type=MESH)
    pl.semaphore_signal(barrier, inc=1, device_id=partner(), device_id_type=MESH)

    load_fields = [
        pltpu.make_async_copy(fields_ref.at[f], term.at[0, f, inner], load_sem.at[f])
        for f in range(FIELDS)
    ]
    load_potential = pltpu.make_async_copy(potential_ref, pot, load_sem.at[FIELDS])
    load_table = pltpu.make_async_copy(projectors_ref, table, load_sem.at[FIELDS + 1])
    load_atoms = [
        pltpu.make_async_copy(src, dst, load_sem.at[FIELDS + 2 + i])
        for i, (src, dst) in enumerate(
            (
                (corners_hbm, corners_ref),
                (counts_hbm, counts_ref),
                (coupling_hbm, coupling_ref),
                (occupations_hbm, occupations_ref),
            )
        )
    ]
    for copy in load_atoms:
        copy.start()
    load_table.start()
    for copy in load_fields:
        copy.start()
    load_potential.start()

    lane = lane_index((1, LANES))
    atom_of_lane = (lane // BOX) % 4

    for copy in load_atoms:
        copy.wait()

    def over_atoms(values):
        values = [jnp.broadcast_to(v, (1, LANES)) for v in values]
        line = jnp.where(atom_of_lane == 0, values[0], values[1])
        line = jnp.where(atom_of_lane == 2, values[2], line)
        return jnp.where(atom_of_lane == 3, values[3], line)

    for axis in range(3):
        line = over_atoms([corners_ref[a : a + 1, axis : axis + 1] for a in range(4)])
        line = line % CELL if axis < 2 else line
        info[axis : axis + 1] = line.astype(f32)
    count = over_atoms([counts_ref[0:1, a : a + 1] for a in range(4)])
    entry = [
        [over_atoms([coupling_ref[a, j : j + 1, i : i + 1] for a in range(4)]) for i in range(NPROJ)]
        for j in range(NPROJ)
    ]
    for i in range(NPROJ):
        for j in range(NPROJ):
            line = jnp.where(count > max(i, j), 0.5 * (entry[j][i] + entry[i][j]), 0.0)
            info[8 + 4 * i + j : 9 + 4 * i + j] = line

    r = row_index((2 * LANES, LANES))
    l = lane_index((2 * LANES, LANES))
    compact[...] = jnp.where((l < PAIR * 16) & (l % 16 == r // 16), 1.0, 0.0).astype(bf16)
    r = row_index((LANES, 2 * LANES))
    l = lane_index((LANES, 2 * LANES))
    expand[...] = jnp.where(r % 16 == l // 16, 1.0, 0.0).astype(bf16)
    fold = jnp.where(
        row_index((LANES, LANES)) % 16 == lane_index((LANES, LANES)) % 16, 1.0, 0.0
    ).astype(bf16)

    def info_copies():
        return [
            pltpu.make_async_remote_copy(
                src_ref=info, dst_ref=info_in.at[i], send_sem=info_send.at[i],
                recv_sem=info_recv.at[i], device_id=peer(*d), device_id_type=MESH,
            )
            for i, d in enumerate(ABOVE)
        ]

    def side_copies(n, g):
        fields = pl.ds(PAIR * g, PAIR)
        copies = []
        for k, d in enumerate(SIDES):
            if k == 0:
                src, dst = term.at[n, fields, pl.ds(CELL, 2)], term.at[n, fields, pl.ds(0, 2)]
            elif k == 1:
                src, dst = term.at[n, fields, pl.ds(2, 2)], term.at[n, fields, pl.ds(CELL + 2, 2)]
            else:
                rows = pl.ds(CELL - 2, 2) if k == 2 else pl.ds(0, 2)
                src, dst = term.at[n, fields, inner, rows], side_y.at[n, fields, :, rows]
            copies.append(
                pltpu.make_async_remote_copy(
                    src_ref=src, dst_ref=dst, send_sem=side_send.at[n, g, k],
                    recv_sem=side_recv.at[n, g, k], device_id=peer(*d), device_id_type=MESH,
                )
            )
        return copies

    def share_copies(n, g):
        return [
            pltpu.make_async_remote_copy(
                src_ref=shares_out.at[n, g, k], dst_ref=shares_in.at[n, g, k],
                send_sem=share_send.at[n, g, k], recv_sem=share_recv.at[n, g, k],
                device_id=peer(*d), device_id_type=MESH,
            )
            for k, d in enumerate(NEAR)
        ]

    pl.semaphore_wait(barrier, len(NEAR) + 1)

    for copy in info_copies():
        copy.start()
    for copy in load_fields:
        copy.wait()
    for g in range(2):
        for copy in side_copies(0, g):
            copy.start()

    load_table.wait()
    own_group = row_index((8, LANES)) == lane_index((8, LANES)) // 16
    for j in range(NPROJ):
        pieces = []
        for c in range(2 * BOX):
            line = table[j : j + 1, c * LANES : (c + 1) * LANES]
            pieces.append(jnp.where(own_group, jnp.broadcast_to(line, (8, LANES)), 0.0))
        boxes[j] = dot_exact(jnp.concatenate(pieces, axis=0), fold).reshape(BOX, BOX, LANES)

    def split_first(x, _):
        for f in range(FIELDS):
            high, low = halves(term[0, f, x + 2])
            split_term[f, x, :, :LANES] = high
            split_term[f, x, :, LANES:] = low
        return 0

    lax.fori_loop(0, CELL, split_first, 0)
    load_potential.wait()

    for copy in info_copies():
        copy.wait_recv()

    upper = lane >= 64
    from_xy, from_x, from_y = (info_in.at[i] for i in range(3))
    near_x = []
    for h in range(2):
        a, b = (info, from_x) if h == 0 else (from_y, from_xy)
        near_x.append(jnp.where(upper, b[...], a[...]))
    for h in range(2):
        depth = (near_x[h][2:3].astype(jnp.int32) + lane % 16) % LANES
        hit = row_index((LANES, LANES)) == depth
        pick = jnp.where(hit, 1.0, 0.0)
        across = pick.T.astype(bf16)
        pick = pick.astype(bf16)
        pick_in[:LANES, h * LANES : (h + 1) * LANES] = pick
        pick_in[LANES:, h * LANES : (h + 1) * LANES] = pick
        pick_out[h * LANES : (h + 1) * LANES] = across
        pick_out[(h + 2) * LANES : (h + 3) * LANES] = across
        for i in range(NPROJ):
            rows = near_x[h][8 + 4 * i : 12 + 4 * i]
            coupled[i, :, h * LANES : (h + 1) * LANES] = jnp.concatenate([rows] * PAIR, axis=0)

    row = row_index((CELL, LANES))
    for h in range(2):
        at_y = near_x[h][1:2].astype(jnp.int32)
        shift = jnp.broadcast_to(at_y if h == 0 else CELL - at_y, (CELL, LANES))
        bits = []
        for b in range(4):
            step = 1 << b
            stays = row >= step if h == 0 else row < CELL - step
            moved = (shift // step) % 2 == 1
            bits.append((step if h == 0 else CELL - step, moved & stays, moved & ~stays))
        whole = shift >= CELL

        def place_y(i, _, bits=bits, whole=whole, h=h):
            for j in range(NPROJ):
                v = boxes[j, i]
                for step, keep, drop in bits:
                    rolled = pltpu.roll(v, step, 0)
                    v = jnp.where(keep, rolled, jnp.where(drop, 0.0, v))
                placed_y[h, j, i] = jnp.where(whole, 0.0, v)
            return 0

        lax.fori_loop(0, BOX, place_y, 0)

    for h in range(2):
        at_x = jnp.broadcast_to(near_x[h][0:1].astype(jnp.int32), (CELL, LANES))
        above = jnp.broadcast_to(upper, (CELL, LANES))
        down = [~above & ((at_x // (1 << b)) % 2 == 1) for b in range(4)]
        up = [above & (((CELL - at_x) // (1 << b)) % 2 == 1) for b in range(4)]
        whole = above & (at_x == 0)

        def place_x(j, _, down=down, up=up, whole=whole, h=h):
            v = [placed_y[h, j, i] for i in range(BOX)]
            zero = jnp.zeros((CELL, LANES), f32)
            for b in range(4):
                step = 1 << b
                v = [
                    jnp.where(
                        down[b],
                        v[x - step] if x >= step else zero,
                        jnp.where(up[b], v[x + step] if x + step < CELL else zero, v[x]),
                    )
                    for x in range(CELL)
                ]
            for x in range(CELL):
                frames[h, j, x] = jnp.where(whole, 0.0, v[x])
            return 0

        lax.fori_loop(0, NPROJ, place_x, 0)

    def send_shares(n, q, g):
        cells = split_term[pl.ds(PAIR * g, PAIR)].reshape(PAIR * CELL * CELL, 2 * LANES)
        slabs[...] = jnp.dot(cells, pick_in[...], preferred_element_type=f32).reshape(slabs.shape)
        sums = []
        for h in range(2):

            def add(x, totals, h=h):
                frame = [frames[h, j, x] for j in range(NPROJ)]
                new = []
                for o in range(PAIR):
                    part = slabs[o, x, :, h * LANES : (h + 1) * LANES]
                    for j in range(NPROJ):
                        product = part * frame[j]
                        new.append(totals[o * NPROJ + j] + product[:8] + product[8:])
                return tuple(new)

            zero = jnp.zeros((8, LANES), f32)
            totals = lax.fori_loop(0, CELL, add, (zero,) * (PAIR * NPROJ), unroll=UNROLL)
            sums.append(jnp.concatenate([jnp.sum(t, axis=0, keepdims=True) for t in totals], axis=0))
        lines = dot_exact(jnp.concatenate(sums, axis=1), compact[...])
        mine = jnp.zeros((NPROJ, LANES), f32)
        lane4 = lane_index((NPROJ, LANES))
        for o in range(PAIR):
            mine = mine + jnp.where(lane4 // 16 == o, lines[4 * o : 4 * o + 4], 0.0)
        shares[q] = mine
        slot = (lane4 // 4) % 4
        valid = lane4 < PAIR * 16
        for k, (dx, dy) in enumerate(NEAR):
            keep = valid
            if dx:
                keep = keep & (slot % 2 == (1 if dx == 1 else 0))
            if dy:
                keep = keep & (slot // 2 == (1 if dy == 1 else 0))
            moved = pltpu.roll(mine, (4 * dx + 8 * dy) % LANES, 1)
            shares_out[n, g, k] = jnp.where(keep, moved, 0.0)
        for copy in share_copies(n, g):
            copy.start()

    for q in range(2):
        send_shares(0, q, q)

    row16 = row_index((CELL, LANES))

    def make_term(n, q, g, store):
        last, other = n - 1, 1 - g
        for copy in side_copies(last, other):
            copy.wait_recv()

        def stencil(x, _):
            v = pot[x]
            for o in range(PAIR):
                f = PAIR * other + o
                u = term[last, f, x + 2]
                edge = side_y[last, f, x]
                near = term[last, f, x + 1] + term[last, f, x + 3]
                far = term[last, f, x] + term[last, f, x + 4]
                near = near + pltpu.roll(jnp.where(row16 == 0, edge, u), CELL - 1, 0)
                near = near + pltpu.roll(jnp.where(row16 == CELL - 1, edge, u), 1, 0)
                far = far + pltpu.roll(jnp.where(row16 < 2, edge, u), CELL - 2, 0)
                far = far + pltpu.roll(jnp.where(row16 >= CELL - 2, edge, u), 2, 0)
                near = near + pltpu.roll(u, 1, 1) + pltpu.roll(u, LANES - 1, 1)
                far = far + pltpu.roll(u, 2, 1) + pltpu.roll(u, LANES - 2, 1)
                local_part[o, x] = (v + 3.75) * u + (-2.0 / 3.0) * near + (1.0 / 24.0) * far
            return 0

        lax.fori_loop(0, CELL, stencil, 0, unroll=UNROLL)

        for copy in share_copies(last, other):
            copy.wait_recv()
        total = shares[q]
        for k in range(len(NEAR)):
            total = total + shares_in[last, other, k]
        rows = PAIR * NPROJ
        field_of_row = row_index((rows, LANES)) // NPROJ
        field_of_lane = lane_index((rows, LANES)) // 16
        lines = [
            jnp.where(
                field_of_row == field_of_lane, jnp.broadcast_to(total[i : i + 1], (rows, LANES)), 0.0
            )
            for i in range(NPROJ)
        ]
        wide = dot_exact(jnp.concatenate(lines, axis=0), expand[...])
        weights = coupled[0] * wide[:rows]
        for i in range(1, NPROJ):
            weights = weights + coupled[i] * wide[i * rows : (i + 1) * rows]
        coef[...] = weights

        for h in range(2):
            lanes = pl.ds(h * LANES, LANES)

            def spread(x, _, h=h, lanes=lanes):
                frame = [frames[h, j, x] for j in range(NPROJ)]
                for o in range(PAIR):
                    value = coef[o * NPROJ : o * NPROJ + 1, lanes] * frame[0]
                    for j in range(1, NPROJ):
                        value = value + coef[o * NPROJ + j : o * NPROJ + j + 1, lanes] * frame[j]
                    high, low = halves(value)
                    split_values[o, x, :, h * LANES : (h + 1) * LANES] = high
                    split_values[o, x, :, (h + 2) * LANES : (h + 3) * LANES] = low
                return 0

            lax.fori_loop(0, CELL, spread, 0, unroll=UNROLL)

        projected[...] = jnp.dot(
            split_values[...].reshape(PAIR * CELL * CELL, 4 * LANES), pick_out[...],
            preferred_element_type=f32,
        ).reshape(projected.shape)
        factor = TIME_STEP / (jnp.zeros((CELL, LANES), f32) + n) * (1 - 2 * g)

        def line(x, _):
            for o in range(PAIR):
                store(PAIR * g + o, x, factor * (local_part[o, x] + projected[o, x]))
            return 0

        lax.fori_loop(0, CELL, line, 0, unroll=UNROLL)

    def step(m, _):
        n, q = m // 2, m % 2
        g = (n + q) % 2

        def store(f, x, value):
            term[n, f, x + 2] = value
            high, low = halves(value)
            split_term[f, x, :, :LANES] = high
            split_term[f, x, :, LANES:] = low

        make_term(n, q, g, store)
        for copy in side_copies(n, g):
            copy.start()
        send_shares(n, q, g)
        return 0

    lax.fori_loop(2, 2 * STEPS, step, 0)

    def store_last(f, x, value):
        total = term[0, f, x + 2] + term[1, f, x + 2]
        propagated_ref[f, x] = total + term[2, f, x + 2] + term[3, f, x + 2] + value

    def finish(q, _):
        make_term(STEPS, q, q, store_last)
        return 0

    lax.fori_loop(0, 2, finish, 0)

    occupied = [jnp.broadcast_to(occupations_ref[0:1, o : o + 1], (CELL, LANES)) for o in range(PAIR)]

    def density(x, _):
        total = jnp.zeros((CELL, LANES), f32)
        for f in range(FIELDS):
            total = total + occupied[f % PAIR] * (propagated_ref[f, x] * propagated_ref[f, x])
        dens[x] = total
        return 0

    lax.fori_loop(0, CELL, density, 0, unroll=UNROLL)
    send = pltpu.make_async_remote_copy(
        src_ref=dens, dst_ref=dens_in, send_sem=dens_send, recv_sem=dens_recv,
        device_id=partner(), device_id_type=MESH,
    )
    send.start()
    for copy in info_copies():
        copy.wait_send()

    def drain(n, _):
        for g in range(2):
            for copy in side_copies(n, g) + share_copies(n, g):
                copy.wait_send()
        return 0

    lax.fori_loop(0, STEPS, drain, 0)
    send.wait_recv()
    density_ref[...] = dens[...] + dens_in[...]
    send.wait_send()


def hand_over(propagated_ref, density_ref, propagated_out, density_out, sem):
    copies = [
        pltpu.make_async_copy(propagated_ref.at[f], propagated_out.at[f], sem.at[f])
        for f in range(FIELDS)
    ]
    copies.append(pltpu.make_async_copy(density_ref, density_out, sem.at[FIELDS]))
    for copy in copies:
        copy.start()
    for copy in copies:
        copy.wait()


def local(orbitals, potential, corners, counts, coupling, projectors, occupations):
    fields = orbitals.reshape(FIELDS, CELL, CELL, LANES)
    vmem = pl.BlockSpec(memory_space=pltpu.VMEM)
    hbm = pl.BlockSpec(memory_space=pltpu.HBM)
    grid = (CELL, CELL, LANES)
    dma = pltpu.SemaphoreType.DMA
    near = len(NEAR)
    propagated, density = pl.pallas_call(
        kernel,
        out_shape=(
            pltpu.VMEM((FIELDS,) + grid, f32),
            pltpu.VMEM(grid, f32),
        ),
        in_specs=[hbm] * 7,
        out_specs=(vmem, vmem),
        scratch_shapes=[
            pltpu.VMEM((STEPS, FIELDS, CELL + 4, CELL, LANES), f32),
            pltpu.VMEM((STEPS, FIELDS) + grid, f32),
            pltpu.VMEM((PAIR,) + grid, f32),
            pltpu.VMEM(grid, f32),
            pltpu.VMEM((NPROJ, BOX * BOX * BOX), f32),
            pltpu.VMEM((4, 3), jnp.int32),
            pltpu.VMEM((1, 4), jnp.int32),
            pltpu.VMEM((4, NPROJ, NPROJ), f32),
            pltpu.VMEM((1, PAIR), f32),
            pltpu.VMEM((24, LANES), f32),
            pltpu.VMEM((3, 24, LANES), f32),
            pltpu.VMEM((NPROJ,) + grid, f32),
            pltpu.VMEM((2, NPROJ) + grid, f32),
            pltpu.VMEM((2, NPROJ) + grid, f32),
            pltpu.VMEM((2 * LANES, 2 * LANES), bf16),
            pltpu.VMEM((4 * LANES, LANES), bf16),
            pltpu.VMEM((2 * LANES, LANES), bf16),
            pltpu.VMEM((LANES, 2 * LANES), bf16),
            pltpu.VMEM((NPROJ, PAIR * NPROJ, 2 * LANES), f32),
            pltpu.VMEM((PAIR * NPROJ, 2 * LANES), f32),
            pltpu.VMEM((FIELDS, CELL, CELL, 2 * LANES), bf16),
            pltpu.VMEM((PAIR, CELL, CELL, 2 * LANES), f32),
            pltpu.VMEM((PAIR, CELL, CELL, 4 * LANES), bf16),
            pltpu.VMEM((PAIR,) + grid, f32),
            pltpu.VMEM((2, NPROJ, LANES), f32),
            pltpu.VMEM((STEPS, 2, near, NPROJ, LANES), f32),
            pltpu.VMEM((STEPS, 2, near, NPROJ, LANES), f32),
            pltpu.VMEM(grid, f32),
            pltpu.VMEM(grid, f32),
            dma((FIELDS + 6,)),
            dma((3,)),
            dma((3,)),
            dma((STEPS, 2, 4)),
            dma((STEPS, 2, 4)),
            dma((STEPS, 2, near)),
            dma((STEPS, 2, near)),
            dma,
            dma,
        ],
        compiler_params=pltpu.CompilerParams(
            collective_id=1, has_side_effects=True, vmem_limit_bytes=VMEM_BYTES
        ),
    )(
        fields, potential, corners, counts[None], coupling, projectors, occupations[None]
    )
    return propagated.reshape(orbitals.shape), density


def solution(mesh):
    placed = (
        P(None, "band", "gx", "gy", None),
        P("gx", "gy", None),
        P(("gx", "gy"), None),
        P(("gx", "gy")),
        P(("gx", "gy"), None, None),
        P(),
        P("band"),
    )
    return jax.shard_map(
        local,
        mesh=mesh,
        in_specs=placed,
        out_specs=(P(None, "band", "gx", "gy", None), P("gx", "gy", None)),
        check_vma=False,
    )
```

time: 70.3 us -> 55.9 us (0.80)
  Pallas kernels: 59.9 us -> 53.7 us
  local copies, waits for them, and re-layouts: 5.88 us -> 1.45 us
  other arithmetic: 3.06 us -> 0 us
    pallas_call x1, Pallas kernels: 59.9 us -> 53.7 us  [local(): pl.pallas_call(kernel, out_shape=(pltpu.VMEM((FIELDS,) + grid, f32), pltp...]
    unnamed x9 -> x2, local copies, waits for them, and re-layouts: 3.96 us -> 1.45 us
    transpose x2 -> x0, other arithmetic: 0.85 us -> none  [the longest x1 0.77 us: atom_lines(): columns = jnp.swapaxes(coupled, 1, 2).reshape(-1, NPROJ * NPROJ)]
    convert_element_type x2 -> x0, other arithmetic: 0.8 us -> none  [the longest x1 0.72 us: atom_lines(): (jnp.arange(NPROJ, dtype=jnp.int32)[None, :] < counts[:, None]).astype(f32)]
    slice x1 -> x0, local copies, waits for them, and re-layouts: 0.75 us -> none  [atom_lines(): corners[:, 2:]]
    broadcast_in_dim x2 -> x0, local copies, waits for them, and re-layouts: 0.73 us -> none  [the longest x1 0.72 us: local(): weights = jnp.broadcast_to(occupations[:, None], (2, LANES))]
    mul x1 -> x0, other arithmetic: 0.72 us -> none  [atom_lines(): coupled = symmetric * active[:, :, None] * active[:, None, :]]
where the time goes in v2:
time: 55.9 us; the launch traced here: 55.8 us
  Pallas kernels  53.7 us (96%)
  local copies, waits for them, and re-layouts  1.45 us (3%)
  between operations  0.64 us (1%)
    pallas_call x1, Pallas kernels, local(): pl.pallas_call(kernel, out_shape=(pltpu.VMEM((FIELDS,) + grid, f32), pltp...  53.7 us
    unnamed x2, local copies, waits for them, and re-layouts  1.45 us

profile of v2, /device:TPU:25, one launch (start us, length us, event | category | flops | bytes accessed | tf_op | source)
XLA Modules:
  0.0 55.8 jit_solution(4084785977295099570)
XLA Ops:
  0.6 53.7 %shard_map.86 = (f32[4,16,16,128]{3,2,1,0:T(8,128)S(1)}, f32[16,16,128]{2,1,0:T(8,128)S(1)}) custom-call(f32[4,16,16,128]{3,2,1,0:T(8,128)} %bitcast.5, f32[16,16,128]{2,1,0:T(8,128)} %potential_ref.1, s32[4,3]{1,0:T(4,128)} %corners_hbm.1, s32[1,4]{1,0:T(1,128)} %bitcast.6, f32[4,4,4]{2,1,0:T(4,128)} %coupling_hbm.1, f32[4,4096]{1,0:T(4,128)} %projectors_ref.1, ...), custom_call_target="tpu_custom_call" | custom-call | tf_op jit(solution)/shard_map/pallas_call | solution.py:476
  54.3 0.8 %copy.11 = f32[2,2,16,16,128]{4,3,2,1,0:T(8,128)} copy(f32[2,2,16,16,128]{4,3,2,1,0:T(8,128)S(1)} %bitcast.4) | data formatting | bytes 1048576
  55.1 0.7 %copy.12 = f32[16,16,128]{2,1,0:T(8,128)} copy(f32[16,16,128]{2,1,0:T(8,128)S(1)} %get-tuple-element.7) | data formatting | bytes 262144

commit v3 on v2

--- a/solution.py
+++ b/solution.py
@@ -12,7 +12,7 @@
 FIELDS = 4
 STEPS = 4
 PAIR = 2
-UNROLL = 4
+UNROLL = 16
 VMEM_BYTES = 60 * 2**20
 TIME_STEP = 0.12
 MESH = pl.DeviceIdType.MESH
@@ -205,7 +205,7 @@
             split_term[f, x, :, LANES:] = low
         return 0
 
-    lax.fori_loop(0, CELL, split_first, 0)
+    lax.fori_loop(0, CELL, split_first, 0, unroll=UNROLL)
     load_potential.wait()
 
     for copy in info_copies():
@@ -252,7 +252,7 @@
                 placed_y[h, j, i] = jnp.where(whole, 0.0, v)
             return 0
 
-        lax.fori_loop(0, BOX, place_y, 0)
+        lax.fori_loop(0, BOX, place_y, 0, unroll=UNROLL)
 
     for h in range(2):
         at_x = jnp.broadcast_to(near_x[h][0:1].astype(jnp.int32), (CELL, LANES))
@@ -278,7 +278,7 @@
                 frames[h, j, x] = jnp.where(whole, 0.0, v[x])
             return 0
 
-        lax.fori_loop(0, NPROJ, place_x, 0)
+        lax.fori_loop(0, NPROJ, place_x, 0, unroll=NPROJ)
 
     def send_shares(n, q, g):
         cells = split_term[pl.ds(PAIR * g, PAIR)].reshape(PAIR * CELL * CELL, 2 * LANES)
@@ -323,7 +323,7 @@
 
     row16 = row_index((CELL, LANES))
 
-    def make_term(n, q, g, store):
+    def make_term(n, q, g, store, spans=((0, CELL),), after=None):
         last, other = n - 1, 1 - g
         for copy in side_copies(last, other):
             copy.wait_recv()
@@ -367,10 +367,11 @@
             weights = weights + coupled[i] * wide[i * rows : (i + 1) * rows]
         coef[...] = weights
 
-        for h in range(2):
-            lanes = pl.ds(h * LANES, LANES)
-
-            def spread(x, _, h=h, lanes=lanes):
+        factor = TIME_STEP / (jnp.zeros((CELL, LANES), f32) + n) * (1 - 2 * g)
+
+        def spread(x, _):
+            for h in range(2):
+                lanes = pl.ds(h * LANES, LANES)
                 frame = [frames[h, j, x] for j in range(NPROJ)]
                 for o in range(PAIR):
                     value = coef[o * NPROJ : o * NPROJ + 1, lanes] * frame[0]
@@ -379,22 +380,23 @@
                     high, low = halves(value)
                     split_values[o, x, :, h * LANES : (h + 1) * LANES] = high
                     split_values[o, x, :, (h + 2) * LANES : (h + 3) * LANES] = low
-                return 0
-
-            lax.fori_loop(0, CELL, spread, 0, unroll=UNROLL)
-
-        projected[...] = jnp.dot(
-            split_values[...].reshape(PAIR * CELL * CELL, 4 * LANES), pick_out[...],
-            preferred_element_type=f32,
-        ).reshape(projected.shape)
-        factor = TIME_STEP / (jnp.zeros((CELL, LANES), f32) + n) * (1 - 2 * g)
+            return 0
 
         def line(x, _):
             for o in range(PAIR):
                 store(PAIR * g + o, x, factor * (local_part[o, x] + projected[o, x]))
             return 0
 
-        lax.fori_loop(0, CELL, line, 0, unroll=UNROLL)
+        for first, end in spans:
+            count = end - first
+            lax.fori_loop(first, end, spread, 0, unroll=count)
+            part = split_values[:, first:end].reshape(PAIR * count * CELL, 4 * LANES)
+            projected[:, first:end] = jnp.dot(
+                part, pick_out[...], preferred_element_type=f32
+            ).reshape(PAIR, count, CELL, LANES)
+            lax.fori_loop(first, end, line, 0, unroll=count)
+            if after is not None:
+                after(first, end)
 
     def step(m, _):
         n, q = m // 2, m % 2
@@ -418,27 +420,29 @@
         total = term[0, f, x + 2] + term[1, f, x + 2]
         propagated_ref[f, x] = total + term[2, f, x + 2] + term[3, f, x + 2] + value
 
-    def finish(q, _):
-        make_term(STEPS, q, q, store_last)
-        return 0
-
-    lax.fori_loop(0, 2, finish, 0)
-
     occupied = [jnp.broadcast_to(occupations_ref[0:1, o : o + 1], (CELL, LANES)) for o in range(PAIR)]
-
-    def density(x, _):
-        total = jnp.zeros((CELL, LANES), f32)
-        for f in range(FIELDS):
-            total = total + occupied[f % PAIR] * (propagated_ref[f, x] * propagated_ref[f, x])
-        dens[x] = total
-        return 0
-
-    lax.fori_loop(0, CELL, density, 0, unroll=UNROLL)
-    send = pltpu.make_async_remote_copy(
-        src_ref=dens, dst_ref=dens_in, send_sem=dens_send, recv_sem=dens_recv,
-        device_id=partner(), device_id_type=MESH,
-    )
-    send.start()
+    middle = CELL // 2
+
+    def density_copy(i):
+        half = pl.ds(i * middle, middle)
+        return pltpu.make_async_remote_copy(
+            src_ref=dens.at[half], dst_ref=dens_in.at[half], send_sem=dens_send.at[i],
+            recv_sem=dens_recv.at[i], device_id=partner(), device_id_type=MESH,
+        )
+
+    def send_density(first, end):
+        def density(x, _):
+            total = jnp.zeros((CELL, LANES), f32)
+            for f in range(FIELDS):
+                total = total + occupied[f % PAIR] * (propagated_ref[f, x] * propagated_ref[f, x])
+            dens[x] = total
+            return 0
+
+        lax.fori_loop(first, end, density, 0, unroll=end - first)
+        density_copy(first // middle).start()
+
+    make_term(STEPS, 0, 0, store_last)
+    make_term(STEPS, 1, 1, store_last, ((0, middle), (middle, CELL)), send_density)
     for copy in info_copies():
         copy.wait_send()
 
@@ -449,9 +453,12 @@
         return 0
 
     lax.fori_loop(0, STEPS, drain, 0)
-    send.wait_recv()
-    density_ref[...] = dens[...] + dens_in[...]
-    send.wait_send()
+    for i in range(2):
+        density_copy(i).wait_recv()
+        half = pl.ds(i * middle, middle)
+        density_ref[half] = dens[half] + dens_in[half]
+    for i in range(2):
+        density_copy(i).wait_send()
 
 
 def hand_over(propagated_ref, density_ref, propagated_out, density_out, sem):
@@ -518,8 +525,8 @@
             dma((STEPS, 2, 4)),
             dma((STEPS, 2, near)),
             dma((STEPS, 2, near)),
-            dma,
-            dma,
+            dma((2,)),
+            dma((2,)),
         ],
         compiler_params=pltpu.CompilerParams(
             collective_id=1, has_side_effects=True, vmem_limit_bytes=VMEM_BYTES
@@ -527,6 +534,17 @@
     )(
         fields, potential, corners, counts[None], coupling, projectors, occupations[None]
     )
+    propagated, density = pl.pallas_call(
+        hand_over,
+        out_shape=(
+            jax.ShapeDtypeStruct((FIELDS,) + grid, f32),
+            jax.ShapeDtypeStruct(grid, f32),
+        ),
+        in_specs=[vmem] * 2,
+        out_specs=(hbm, hbm),
+        scratch_shapes=[dma((FIELDS + 1,))],
+        compiler_params=pltpu.CompilerParams(vmem_limit_bytes=2**20),
+    )(propagated, density)
     return propagated.reshape(orbitals.shape), density
 
 

time: 55.9 us -> 52.9 us (0.946)
  Pallas kernels: 53.7 us -> 52.2 us
  local copies, waits for them, and re-layouts: 1.45 us -> 0 us
    pallas_call x1, Pallas kernels: 53.7 us -> 51.3 us  [local(): pl.pallas_call(kernel, out_shape=(pltpu.VMEM((FIELDS,) + grid, f32), pltp...]
    unnamed x2 -> x0, local copies, waits for them, and re-layouts: 1.45 us -> none
    pallas_call x0 -> x1, Pallas kernels: none -> 0.87 us  [local(): pl.pallas_call(hand_over, out_shape=(jax.ShapeDtypeStruct((FIELDS,) + gri...]
where the time goes in v3:
time: 52.9 us; the launch traced here: 52.8 us
  Pallas kernels  52.2 us (99%)
  between operations  0.64 us (1%)
    pallas_call x1, Pallas kernels, local(): pl.pallas_call(kernel, out_shape=(pltpu.VMEM((FIELDS,) + grid, f32), pltp...  51.3 us

profile of v3, /device:TPU:25, one launch (start us, length us, event | category | flops | bytes accessed | tf_op | source)
XLA Modules:
  0.0 52.8 jit_solution(11722248588334765663)
XLA Ops:
  0.6 51.3 %shard_map.86 = (f32[4,16,16,128]{3,2,1,0:T(8,128)S(1)}, f32[16,16,128]{2,1,0:T(8,128)S(1)}) custom-call(f32[4,16,16,128]{3,2,1,0:T(8,128)} %bitcast.4, f32[16,16,128]{2,1,0:T(8,128)} %potential_ref.1, s32[4,3]{1,0:T(4,128)} %corners_hbm.1, s32[1,4]{1,0:T(1,128)} %bitcast.5, f32[4,4,4]{2,1,0:T(4,128)} %coupling_hbm.1, f32[4,4096]{1,0:T(4,128)} %projectors_ref.1, ...), custom_call_target="tpu_custom_call" | custom-call | tf_op jit(solution)/shard_map/pallas_call | solution.py:483
  51.9 0.9 %shard_map.87 = (f32[4,16,16,128]{3,2,1,0:T(8,128)}, f32[16,16,128]{2,1,0:T(8,128)}) custom-call(f32[4,16,16,128]{3,2,1,0:T(8,128)S(1)} %get-tuple-element.6.propagated_ref, f32[16,16,128]{2,1,0:T(8,128)S(1)} %get-tuple-element.7.density_ref), custom_call_target="tpu_custom_call" | custom-call | tf_op jit(solution)/shard_map/pallas_call | solution.py:537

commit v4 on v3

--- a/solution.py
+++ b/solution.py
@@ -208,17 +208,19 @@
     lax.fori_loop(0, CELL, split_first, 0, unroll=UNROLL)
     load_potential.wait()
 
-    for copy in info_copies():
-        copy.wait_recv()
-
     upper = lane >= 64
+    row = row_index((CELL, LANES))
+    above = jnp.broadcast_to(upper, (CELL, LANES))
+    zero = jnp.zeros((CELL, LANES), f32)
+    arrivals = info_copies()
     from_xy, from_x, from_y = (info_in.at[i] for i in range(3))
-    near_x = []
     for h in range(2):
-        a, b = (info, from_x) if h == 0 else (from_y, from_xy)
-        near_x.append(jnp.where(upper, b[...], a[...]))
-    for h in range(2):
-        depth = (near_x[h][2:3].astype(jnp.int32) + lane % 16) % LANES
+        for i in (1,) if h == 0 else (2, 0):
+            arrivals[i].wait_recv()
+        low, high = (info, from_x) if h == 0 else (from_y, from_xy)
+        atoms = jnp.where(upper, high[...], low[...])
+
+        depth = (atoms[2:3].astype(jnp.int32) + lane % 16) % LANES
         hit = row_index((LANES, LANES)) == depth
         pick = jnp.where(hit, 1.0, 0.0)
         across = pick.T.astype(bf16)
@@ -228,12 +230,10 @@
         pick_out[h * LANES : (h + 1) * LANES] = across
         pick_out[(h + 2) * LANES : (h + 3) * LANES] = across
         for i in range(NPROJ):
-            rows = near_x[h][8 + 4 * i : 12 + 4 * i]
+            rows = atoms[8 + 4 * i : 12 + 4 * i]
             coupled[i, :, h * LANES : (h + 1) * LANES] = jnp.concatenate([rows] * PAIR, axis=0)
 
-    row = row_index((CELL, LANES))
-    for h in range(2):
-        at_y = near_x[h][1:2].astype(jnp.int32)
+        at_y = atoms[1:2].astype(jnp.int32)
         shift = jnp.broadcast_to(at_y if h == 0 else CELL - at_y, (CELL, LANES))
         bits = []
         for b in range(4):
@@ -242,28 +242,20 @@
             moved = (shift // step) % 2 == 1
             bits.append((step if h == 0 else CELL - step, moved & stays, moved & ~stays))
         whole = shift >= CELL
-
-        def place_y(i, _, bits=bits, whole=whole, h=h):
+        for i in range(BOX):
             for j in range(NPROJ):
                 v = boxes[j, i]
                 for step, keep, drop in bits:
                     rolled = pltpu.roll(v, step, 0)
                     v = jnp.where(keep, rolled, jnp.where(drop, 0.0, v))
-                placed_y[h, j, i] = jnp.where(whole, 0.0, v)
-            return 0
-
-        lax.fori_loop(0, BOX, place_y, 0, unroll=UNROLL)
-
-    for h in range(2):
-        at_x = jnp.broadcast_to(near_x[h][0:1].astype(jnp.int32), (CELL, LANES))
-        above = jnp.broadcast_to(upper, (CELL, LANES))
+                placed_y[h, j, i] = jnp.where(whole, 0.0, v) if h else v
+
+        at_x = jnp.broadcast_to(atoms[0:1].astype(jnp.int32), (CELL, LANES))
         down = [~above & ((at_x // (1 << b)) % 2 == 1) for b in range(4)]
         up = [above & (((CELL - at_x) // (1 << b)) % 2 == 1) for b in range(4)]
-        whole = above & (at_x == 0)
-
-        def place_x(j, _, down=down, up=up, whole=whole, h=h):
+        outside = above & (at_x == 0)
+        for j in range(NPROJ):
             v = [placed_y[h, j, i] for i in range(BOX)]
-            zero = jnp.zeros((CELL, LANES), f32)
             for b in range(4):
                 step = 1 << b
                 v = [
@@ -275,10 +267,7 @@
                     for x in range(CELL)
                 ]
             for x in range(CELL):
-                frames[h, j, x] = jnp.where(whole, 0.0, v[x])
-            return 0
-
-        lax.fori_loop(0, NPROJ, place_x, 0, unroll=NPROJ)
+                frames[h, j, x] = jnp.where(outside, 0.0, v[x])
 
     def send_shares(n, q, g):
         cells = split_term[pl.ds(PAIR * g, PAIR)].reshape(PAIR * CELL * CELL, 2 * LANES)

time: 52.9 us -> 52.3 us (0.989)
  Pallas kernels: 52.2 us -> 51.5 us
    pallas_call x1, Pallas kernels: 51.3 us -> 50.7 us  [local(): pl.pallas_call(kernel, out_shape=(pltpu.VMEM((FIELDS,) + grid, f32), pltp...]
where the time goes in v4:
time: 52.3 us; the launch traced here: 52.2 us
  Pallas kernels  51.5 us (98%)
  between operations  0.64 us (1%)
    pallas_call x1, Pallas kernels, local(): pl.pallas_call(kernel, out_shape=(pltpu.VMEM((FIELDS,) + grid, f32), pltp...  50.7 us

profile of v4, /device:TPU:25, one launch (start us, length us, event | category | flops | bytes accessed | tf_op | source)
XLA Modules:
  0.0 52.2 jit_solution(11815336894415980343)
XLA Ops:
  0.6 50.7 %shard_map.86 = (f32[4,16,16,128]{3,2,1,0:T(8,128)S(1)}, f32[16,16,128]{2,1,0:T(8,128)S(1)}) custom-call(f32[4,16,16,128]{3,2,1,0:T(8,128)} %bitcast.4, f32[16,16,128]{2,1,0:T(8,128)} %potential_ref.1, s32[4,3]{1,0:T(4,128)} %corners_hbm.1, s32[1,4]{1,0:T(1,128)} %bitcast.5, f32[4,4,4]{2,1,0:T(4,128)} %coupling_hbm.1, f32[4,4096]{1,0:T(4,128)} %projectors_ref.1, ...), custom_call_target="tpu_custom_call" | custom-call | tf_op jit(solution)/shard_map/pallas_call | solution.py:472
  51.3 0.9 %shard_map.87 = (f32[4,16,16,128]{3,2,1,0:T(8,128)}, f32[16,16,128]{2,1,0:T(8,128)}) custom-call(f32[4,16,16,128]{3,2,1,0:T(8,128)S(1)} %get-tuple-element.6.propagated_ref, f32[16,16,128]{2,1,0:T(8,128)S(1)} %get-tuple-element.7.density_ref), custom_call_target="tpu_custom_call" | custom-call | tf_op jit(solution)/shard_map/pallas_call | solution.py:526

commit v5 on v4

--- a/solution.py
+++ b/solution.py
@@ -208,6 +208,22 @@
     lax.fori_loop(0, CELL, split_first, 0, unroll=UNROLL)
     load_potential.wait()
 
+    def half_sum(h, at):
+        def add(x, totals):
+            frame = [frames[h, j, x] for j in range(NPROJ)]
+            new = []
+            for o in range(PAIR):
+                part = slabs[o, x, :, at * LANES : (at + 1) * LANES]
+                for j in range(NPROJ):
+                    product = part * frame[j]
+                    new.append(totals[o * NPROJ + j] + product[:8] + product[8:])
+            return tuple(new)
+
+        nothing = jnp.zeros((8, LANES), f32)
+        totals = lax.fori_loop(0, CELL, add, (nothing,) * (PAIR * NPROJ), unroll=UNROLL)
+        return jnp.concatenate(totals, axis=0)
+
+    first_sums = [[], []]
     upper = lane >= 64
     row = row_index((CELL, LANES))
     above = jnp.broadcast_to(upper, (CELL, LANES))
@@ -269,30 +285,30 @@
             for x in range(CELL):
                 frames[h, j, x] = jnp.where(outside, 0.0, v[x])
 
-    def send_shares(n, q, g):
+        for g in range(2):
+            cells = split_term[pl.ds(PAIR * g, PAIR)].reshape(PAIR * CELL * CELL, 2 * LANES)
+            slabs[:, :, :, g * LANES : (g + 1) * LANES] = jnp.dot(
+                cells, pick_in[:, h * LANES : (h + 1) * LANES], preferred_element_type=f32
+            ).reshape(PAIR, CELL, CELL, LANES)
+            first_sums[g].append(half_sum(h, g))
+
+    def inner_products(g):
         cells = split_term[pl.ds(PAIR * g, PAIR)].reshape(PAIR * CELL * CELL, 2 * LANES)
         slabs[...] = jnp.dot(cells, pick_in[...], preferred_element_type=f32).reshape(slabs.shape)
-        sums = []
-        for h in range(2):
-
-            def add(x, totals, h=h):
-                frame = [frames[h, j, x] for j in range(NPROJ)]
-                new = []
-                for o in range(PAIR):
-                    part = slabs[o, x, :, h * LANES : (h + 1) * LANES]
-                    for j in range(NPROJ):
-                        product = part * frame[j]
-                        new.append(totals[o * NPROJ + j] + product[:8] + product[8:])
-                return tuple(new)
-
-            zero = jnp.zeros((8, LANES), f32)
-            totals = lax.fori_loop(0, CELL, add, (zero,) * (PAIR * NPROJ), unroll=UNROLL)
-            sums.append(jnp.concatenate([jnp.sum(t, axis=0, keepdims=True) for t in totals], axis=0))
+        return [half_sum(h, h) for h in range(2)]
+
+    def send_shares(n, q, g, sums):
         lines = dot_exact(jnp.concatenate(sums, axis=1), compact[...])
-        mine = jnp.zeros((NPROJ, LANES), f32)
         lane4 = lane_index((NPROJ, LANES))
-        for o in range(PAIR):
-            mine = mine + jnp.where(lane4 // 16 == o, lines[4 * o : 4 * o + 4], 0.0)
+        group = lane_index((8, LANES)) // 16
+        mine = []
+        for j in range(NPROJ):
+            both = jnp.zeros((8, LANES), f32)
+            for o in range(PAIR):
+                at = 8 * (o * NPROJ + j)
+                both = both + jnp.where(group == o, lines[at : at + 8], 0.0)
+            mine.append(jnp.sum(both, axis=0, keepdims=True))
+        mine = jnp.concatenate(mine, axis=0)
         shares[q] = mine
         slot = (lane4 // 4) % 4
         valid = lane4 < PAIR * 16
@@ -308,7 +324,7 @@
             copy.start()
 
     for q in range(2):
-        send_shares(0, q, q)
+        send_shares(0, q, q, first_sums[q])
 
     row16 = row_index((CELL, LANES))
 
@@ -400,7 +416,7 @@
         make_term(n, q, g, store)
         for copy in side_copies(n, g):
             copy.start()
-        send_shares(n, q, g)
+        send_shares(n, q, g, inner_products(g))
         return 0
 
     lax.fori_loop(2, 2 * STEPS, step, 0)

time: 52.3 us -> 52.3 us (level)
  no operation moved by 1% of the time
where the time goes in v5:
time: 52.3 us; the launch traced here: 52.2 us
  Pallas kernels  51.5 us (98%)
  between operations  0.64 us (1%)
    pallas_call x1, Pallas kernels, local(): pl.pallas_call(kernel, out_shape=(pltpu.VMEM((FIELDS,) + grid, f32), pltp...  50.7 us

profile of v5, /device:TPU:25, one launch (start us, length us, event | category | flops | bytes accessed | tf_op | source)
XLA Modules:
  0.0 52.2 jit_solution(852589741534016361)
XLA Ops:
  0.6 50.7 %shard_map.86 = (f32[4,16,16,128]{3,2,1,0:T(8,128)S(1)}, f32[16,16,128]{2,1,0:T(8,128)S(1)}) custom-call(f32[4,16,16,128]{3,2,1,0:T(8,128)} %bitcast.4, f32[16,16,128]{2,1,0:T(8,128)} %potential_ref.1, s32[4,3]{1,0:T(4,128)} %corners_hbm.1, s32[1,4]{1,0:T(1,128)} %bitcast.5, f32[4,4,4]{2,1,0:T(4,128)} %coupling_hbm.1, f32[4,4096]{1,0:T(4,128)} %projectors_ref.1, ...), custom_call_target="tpu_custom_call" | custom-call | tf_op jit(solution)/shard_map/pallas_call | solution.py:488
  51.3 0.9 %shard_map.87 = (f32[4,16,16,128]{3,2,1,0:T(8,128)}, f32[16,16,128]{2,1,0:T(8,128)}) custom-call(f32[4,16,16,128]{3,2,1,0:T(8,128)S(1)} %get-tuple-element.6.propagated_ref, f32[16,16,128]{2,1,0:T(8,128)S(1)} %get-tuple-element.7.density_ref), custom_call_target="tpu_custom_call" | custom-call | tf_op jit(solution)/shard_map/pallas_call | solution.py:542
